TPU v7x, 32 devices: a whole 2x2x4 slice. The times are simulated.
32 devices in a mesh: tm: 4 (over y, x), space: 8 (over z, core).
Axes of the slice: x: 2, y: 2, z: 4, core: 2. Of those that a mesh axis runs over, the one named last changes fastest.
Arguments:
- activations: bfloat16 [32, 16, 8, 1024], P('tm', 'space'), may hold values from -6 to 6
- in_proj: bfloat16 [1024, 2176], replicated, may hold values from -0.1875 to 0.1875
- step_proj: bfloat16 [1024, 16], replicated, may hold values from -0.1875 to 0.1875
- step_bias: float32 [16], replicated, may hold values from -2 to 0
- decay_rates: float32 [16], replicated, may hold values from 0.005 to 0.5
- conv_kernel: float32 [3, 3, 1152], replicated, may hold values from -2 to 2
- conv_bias: float32 [1152], replicated, may hold values from -3 to 3
- skip_gain: float32 [16], replicated, may hold values from 0.5 to 1.5
- norm_gain: float32 [1024], replicated, may hold values from 0.5 to 1.5
- out_proj: bfloat16 [1024, 1024], replicated, may hold values from -0.1875 to 0.1875
- out_cotangent: bfloat16 [32, 16, 8, 1024], P('tm', 'space'), may hold values from -6 to 6
Outputs:
- layer_out: bfloat16 [32, 16, 8, 1024], P('tm', 'space')
- grad_input: bfloat16 [32, 16, 8, 1024], P('tm', 'space')
- grad_in_proj: float32 [1024, 2176], P(('tm', 'space'))
- grad_step_proj: float32 [1024, 16], P(('tm', 'space'))
- grad_out_proj_t: float32 [1024, 1024], P(('tm', 'space'))
- grad_conv_kernel: float32 [3, 3, 1152], replicated
- grad_conv_bias: float32 [1152], replicated
- grad_step_bias: float32 [16], replicated
- grad_decay_rates: float32 [16], replicated
- grad_skip_gain: float32 [16], replicated
- grad_norm_gain: float32 [1024], replicated
All inputs are finite; a program needn't handle non-finite values.
Results may differ from a plain program's by a relative error of at most 0.015.
The roundings to bfloat16 on the way count: a program that leaves them out, or rounds other values in their place, can miss the bound.
Values may be sent and summed in bfloat16 or wider, within the bound.
A program may use at most 192 MiB of HBM per device.

v0:
```python
import jax
import jax.numpy as jnp
from jax import lax
from jax.sharding import PartitionSpec as P

top_precision = lax.Precision.HIGHEST
norm_eps = 1e-05


def padded_2(block, sides, width):
    for axis, dim in sides:
        count = lax.axis_size(axis)
        forward = [(i, i + 1) for i in range(count - 1)]
        backward = [(target, source) for source, target in forward]
        low = lax.ppermute(
            lax.slice_in_dim(block, block.shape[dim] - width, None, axis=dim), axis, forward
        )
        high = lax.ppermute(lax.slice_in_dim(block, 0, width, axis=dim), axis, backward)
        block = jnp.concatenate([low, block, high], axis=dim)
    return block


def ssd_block(heads_in, b_proj, c_proj, step_in, rate_in, gain_in, state_in):
    decay_step = step_in * rate_in
    running = jnp.cumsum(decay_step, axis=0)
    places = jnp.arange(heads_in.shape[0])
    causal = (places[:, None] >= places[None, :])[:, :, None, None]
    spread = running[:, None] - running[None, :]
    weights = jnp.where(causal, jnp.exp(-jnp.where(causal, spread, 0.0)), 0.0) * step_in[None, :]
    inner_cb = jnp.einsum("tkn,skn->tsk", c_proj, b_proj, precision=top_precision)
    intra_part = jnp.einsum(
        "tskh,skhp->tkhp", weights * inner_cb[..., None], heads_in, precision=top_precision
    )
    carried = jnp.exp(-running)[..., None] * jnp.einsum(
        "tkn,khpn->tkhp", c_proj, state_in, precision=top_precision
    )
    result = intra_part + carried + gain_in[:, None] * heads_in
    final_sum = running[-1]
    tail_weight = jnp.exp(running - final_sum[None]) * step_in
    state_out = jnp.exp(-final_sum)[..., None, None] * state_in + jnp.einsum(
        "skh,skhp,skn->khpn", tail_weight, heads_in, b_proj, precision=top_precision
    )
    return (result, state_out)


def ssd_sequence(heads_in, b_proj, c_proj, step_in, rate_in, gain_in, block_len):
    block_count = heads_in.shape[0] // block_len

    def fold_blocks(array_in):
        return array_in.reshape((block_count, block_len) + array_in.shape[1:])

    start_state = jnp.zeros(heads_in.shape[1:4] + (b_proj.shape[2],), jnp.float32)

    def advance(carry_state, pieces):
        result, carry_state = ssd_block(
            pieces[0], pieces[1], pieces[2], pieces[3], rate_in, gain_in, carry_state
        )
        return (carry_state, result)

    final_state, results = lax.scan(
        advance,
        start_state,
        (fold_blocks(heads_in), fold_blocks(b_proj), fold_blocks(c_proj), fold_blocks(step_in)),
    )
    return (results.reshape(heads_in.shape), final_state)


def gate_norm(ssd_float, gate_float, norm_gain):
    gated = ssd_float * jax.nn.silu(gate_float)
    scale_row = lax.rsqrt(jnp.mean(gated * gated, axis=-1, keepdims=True) + norm_eps)
    return gated * scale_row * norm_gain


def silu_slope(before):
    squashed = jax.nn.sigmoid(before)
    return squashed * (1.0 + before * (1.0 - squashed))


def conv_apply(padded, conv_kernel, conv_bias, row_count, col_count):
    accum = conv_kernel[0, 0] * padded[:, 0:row_count, 0:col_count]
    for row_off in range(3):
        for col_off in range(3):
            if row_off + col_off > 0:
                accum = (
                    accum
                    + conv_kernel[row_off, col_off]
                    * padded[:, row_off : row_off + row_count, col_off : col_off + col_count]
                )
    return accum + conv_bias


def conv_transpose(d_padded, conv_kernel, row_count, col_count):
    accum = conv_kernel[0, 0] * d_padded[:, 2 : 2 + row_count, 2 : 2 + col_count]
    for row_off in range(3):
        for col_off in range(3):
            if row_off + col_off > 0:
                accum = (
                    accum
                    + conv_kernel[row_off, col_off]
                    * d_padded[
                        :,
                        2 - row_off : 2 - row_off + row_count,
                        2 - col_off : 2 - col_off + col_count,
                    ]
                )
    return accum


def kernel_grad(d_before, padded, row_count, col_count):
    parts = []
    for row_off in range(3):
        for col_off in range(3):
            parts.append(
                jnp.sum(
                    d_before
                    * padded[:, row_off : row_off + row_count, col_off : col_off + col_count],
                    axis=(0, 1, 2),
                )
            )
    return jnp.stack(parts).reshape(3, 3, -1)


def on_device(
    activations,
    in_proj,
    step_proj,
    step_bias,
    decay_rates,
    conv_kernel,
    conv_bias,
    skip_gain,
    norm_gain,
    out_proj,
    out_cotangent,
):
    frame_count, row_count, col_count, model_width = activations.shape
    inner_w = out_proj.shape[0]
    head_count = step_proj.shape[1]
    head_dim = inner_w // head_count
    proj_cols = in_proj.shape[1]
    state_n = (proj_cols - 2 * inner_w) // 2
    token_count = row_count * col_count
    flat_act = activations.reshape(-1, model_width)
    projected = jnp.dot(flat_act, in_proj, preferred_element_type=jnp.float32)
    gate_z = projected[:, :inner_w].astype(jnp.bfloat16)
    mixed_in = (
        projected[:, inner_w:].astype(jnp.bfloat16).reshape(frame_count, row_count, col_count, -1)
    )
    step_raw = jnp.dot(flat_act, step_proj, preferred_element_type=jnp.float32) + step_bias
    step_sizes = jax.nn.softplus(step_raw).astype(jnp.bfloat16)
    halo_rows = padded_2(mixed_in, (("space", 1),), 1)
    padded = jnp.pad(halo_rows.astype(jnp.float32), ((0, 0), (0, 0), (1, 1), (0, 0)))
    before = conv_apply(padded, conv_kernel, conv_bias, row_count, col_count)
    activated = jax.nn.silu(before).astype(jnp.bfloat16).reshape(frame_count, token_count, -1)
    steps_tok = step_sizes.reshape(frame_count, token_count, head_count)
    moved_act, moved_steps = (
        lax.all_to_all(activated, "tm", split_axis=1, concat_axis=0, tiled=True),
        lax.all_to_all(steps_tok, "tm", split_axis=1, concat_axis=0, tiled=True),
    )
    all_frames = moved_act.shape[0]
    few_tokens = moved_act.shape[1]
    act_float = moved_act.astype(jnp.float32)
    heads_in = act_float[..., :inner_w].reshape(all_frames, few_tokens, head_count, head_dim)
    heads_in, b_proj, c_proj = (
        heads_in,
        act_float[..., inner_w : inner_w + state_n],
        act_float[..., inner_w + state_n :],
    )

    def ssd_whole(heads_arg, b_arg, c_arg, step_arg, rate_arg, gain_arg):
        return ssd_sequence(heads_arg, b_arg, c_arg, step_arg, rate_arg, gain_arg, frame_count)

    (ssd_float, final_state), pull_back = jax.vjp(
        ssd_whole, heads_in, b_proj, c_proj, moved_steps.astype(jnp.float32), decay_rates, skip_gain
    )
    returned = lax.all_to_all(
        ssd_float.astype(jnp.bfloat16).reshape(all_frames, few_tokens, inner_w),
        "tm",
        split_axis=0,
        concat_axis=1,
        tiled=True,
    )
    ssd_out = returned.reshape(frame_count * token_count, inner_w)
    normed_float, pull_norm = jax.vjp(
        gate_norm, ssd_out.astype(jnp.float32), gate_z.astype(jnp.float32), norm_gain
    )
    normed = normed_float.astype(jnp.bfloat16)
    layer_out = (
        jnp.dot(normed, out_proj, preferred_element_type=jnp.float32)
        .astype(jnp.bfloat16)
        .reshape(activations.shape)
    )
    contract_rows = (((0,), (0,)), ((), ()))
    contract_cols = (((1,), (1,)), ((), ()))
    cot_flat = out_cotangent.reshape(-1, model_width)
    d_normed = lax.dot_general(
        cot_flat, out_proj, contract_cols, preferred_element_type=jnp.float32
    )
    d_ssd, d_gate, norm_part = pull_norm(d_normed)
    d_ssd = d_ssd.astype(jnp.bfloat16)
    moved_grad = lax.all_to_all(
        d_ssd.reshape(frame_count, token_count, inner_w),
        "tm",
        split_axis=1,
        concat_axis=0,
        tiled=True,
    )
    d_result = moved_grad.astype(jnp.float32).reshape(all_frames, few_tokens, head_count, head_dim)
    gradients = pull_back((d_result, jnp.zeros_like(final_state)))
    d_act_seq = jnp.concatenate(
        [gradients[0].reshape(all_frames, few_tokens, inner_w), gradients[1], gradients[2]], axis=-1
    ).astype(jnp.bfloat16)
    d_steps_seq = gradients[3].astype(jnp.bfloat16)
    d_act, d_steps = (
        lax.all_to_all(d_act_seq, "tm", split_axis=0, concat_axis=1, tiled=True),
        lax.all_to_all(d_steps_seq, "tm", split_axis=0, concat_axis=1, tiled=True),
    )
    rate_part = gradients[4]
    gain_part = gradients[5]
    d_before = d_act.astype(jnp.float32).reshape(
        frame_count, row_count, col_count, -1
    ) * silu_slope(before)
    d_rows = padded_2(d_before.astype(jnp.bfloat16), (("space", 1),), 1).astype(d_before.dtype)
    d_padded = jnp.pad(d_rows, ((0, 0), (0, 0), (1, 1), (0, 0)))
    d_mixed = conv_transpose(d_padded, conv_kernel, row_count, col_count)
    kernel_part = kernel_grad(d_before, padded, row_count, col_count)
    conv_bias_part = jnp.sum(d_before, axis=(0, 1, 2))
    d_raw = d_steps.astype(jnp.float32).reshape(-1, head_count) * jax.nn.sigmoid(step_raw)
    bias_part = jnp.sum(d_raw, axis=0)
    d_raw_half = d_raw.astype(jnp.bfloat16)
    d_projected = jnp.concatenate([d_gate, d_mixed.reshape(-1, d_mixed.shape[-1])], axis=1).astype(
        jnp.bfloat16
    )
    grad_input = (
        (
            lax.dot_general(d_projected, in_proj, contract_cols, preferred_element_type=jnp.float32)
            + lax.dot_general(
                d_raw_half, step_proj, contract_cols, preferred_element_type=jnp.float32
            )
        )
        .astype(jnp.bfloat16)
        .reshape(activations.shape)
    )
    summed = lax.psum_scatter(
        jnp.concatenate(
            [
                lax.dot_general(
                    flat_act, d_projected, contract_rows, preferred_element_type=jnp.float32
                ),
                lax.dot_general(
                    cot_flat, normed, contract_rows, preferred_element_type=jnp.float32
                ),
                lax.dot_general(
                    flat_act, d_raw_half, contract_rows, preferred_element_type=jnp.float32
                ),
            ],
            axis=1,
        ),
        ("tm", "space"),
        scatter_dimension=0,
        tiled=True,
    )
    grad_in_proj = summed[:, :proj_cols]
    grad_out_proj_t = summed[:, proj_cols : proj_cols + inner_w]
    grad_step_proj = summed[:, proj_cols + inner_w :]
    small_sums = lax.psum(
        (kernel_part, conv_bias_part, bias_part, rate_part, gain_part, norm_part), ("tm", "space")
    )
    return (
        layer_out,
        grad_input,
        grad_in_proj,
        grad_step_proj,
        grad_out_proj_t,
        small_sums[0],
        small_sums[1],
        small_sums[2],
        small_sums[3],
        small_sums[4],
        small_sums[5],
    )


def solution(mesh):
    placed = (
        P("tm", "space", None, None),
        P(),
        P(),
        P(),
        P(),
        P(),
        P(),
        P(),
        P(),
        P(),
        P("tm", "space", None, None),
    )
    return jax.shard_map(
        on_device,
        mesh=mesh,
        in_specs=placed,
        out_specs=(
            P("tm", "space", None, None),
            P("tm", "space", None, None),
            P(("tm", "space"), None),
            P(("tm", "space"), None),
            P(("tm", "space"), None),
            P(),
            P(),
            P(),
            P(),
            P(),
            P(),
        ),
        check_vma=False,
    )
```

profile of v0, /device:TPU:0, one launch (start us, length us, event | category | flops | bytes accessed | tf_op | source)
XLA Modules:
  0.0 662.4 jit_solution(6901079063649847948)
XLA Ops:
  7.2 3.3 convolution_convert_fusion
  17.6 4.5 all-to-all-start
  23.4 3.4 all-to-all-done
  29.6 4.3 all-to-all-start.1
  34.5 6.1 all-to-all-done.1
  51.1 122.4 %while.77 = (s32[]{:T(128)}, f32[4,16,64,64]{3,2,1,0:T(8,128)}, bf16[4,8,4,16,64]{4,1,3,2,0:T(8,128)(2,1)}, f32[4,8,8,4,16]{2,1,4,3,0:T(8,128)}, f32[4,1,8,4,16]...) while((s32[]{:T(128)}, f32[4,16,64,64]{3,2,1,0:T(8,128)}, ...), condition=%wide.region_2.3_spmd.clone.clone.clone, body=%wide.region_0.2_spmd.clone.clone.sunk.clone | while | flops 55238336 | bytes 13394481 | solution.py:60
  57.5 6.5 bitcast_dynamic-update-slice_fusion.22
  65.6 6.1 multiply_add_fusion.7
  85.7 7.4 %bitcast_dynamic-update-slice_fusion.22 = (f32[4,8,4,16,64]{4,1,3,2,0:T(8,128)}, f32[4,8,16,64]{3,1,2,0:T(8,128)}) fusion(f32[4,8,4,16,64]{4,1,3,2,0:T(8,128)} %get-tuple-element.2468, s32[]{:T(128)} %get-tuple-element.2457, f32[4,16,64,64]{3,2,1,0:T(8,128)} %get-tuple-element.2458, pred[]{:T(512)S(6)} %compare.11, ...), kind=kOutput, calls=%fused_computation.13.clone.1.clone | convolution fusion | flops 25427968 | bytes 2638849 | tf_op jit(solution)/shard_map/jvp()/while/body/eval_jaxpr/tkn,khpn->tkhp/dot_general | solution.py:34
  93.1 3.2 bitcast_dynamic-update-slice_fusion.25
  96.2 6.9 %multiply_add_fusion.7 = f32[4,16,64,64]{3,2,1,0:T(8,128)} fusion(f32[4,16,64,64]{3,2,1,0:T(8,128)} %get-tuple-element.2458, f32[4,16]{1,0:T(4,128)S(1)} %negate_exponential_fusion.8, pred[]{:T(512)S(6)} %compare.11, f32[4,8,4,16,64]{4,1,3,2,0:T(8,128)} %get-tuple-element.2502, s32[]{:T(128)} %get-tuple-element.2457, ...), kind=kOutput, calls=%fused_computation.3.clone.1.clone | convolution fusion | flops 25985024 | bytes 3427585 | tf_op jit(solution)/shard_map/jvp()/while/body/eval_jaxpr/skh,skhp,skn->khpn/dot_general | solution.py:40
  117.0 7.4 %bitcast_dynamic-update-slice_fusion.22 = (f32[4,8,4,16,64]{4,1,3,2,0:T(8,128)}, f32[4,8,16,64]{3,1,2,0:T(8,128)}) fusion(f32[4,8,4,16,64]{4,1,3,2,0:T(8,128)} %get-tuple-element.2468, s32[]{:T(128)} %get-tuple-element.2457, f32[4,16,64,64]{3,2,1,0:T(8,128)} %get-tuple-element.2458, pred[]{:T(512)S(6)} %compare.11, ...), kind=kOutput, calls=%fused_computation.13.clone.1.clone | convolution fusion | flops 25427968 | bytes 2638849 | tf_op jit(solution)/shard_map/jvp()/while/body/eval_jaxpr/tkn,khpn->tkhp/dot_general | solution.py:34
  124.4 3.2 bitcast_dynamic-update-slice_fusion.25
  127.6 6.9 %multiply_add_fusion.7 = f32[4,16,64,64]{3,2,1,0:T(8,128)} fusion(f32[4,16,64,64]{3,2,1,0:T(8,128)} %get-tuple-element.2458, f32[4,16]{1,0:T(4,128)S(1)} %negate_exponential_fusion.8, pred[]{:T(512)S(6)} %compare.11, f32[4,8,4,16,64]{4,1,3,2,0:T(8,128)} %get-tuple-element.2502, s32[]{:T(128)} %get-tuple-element.2457, ...), kind=kOutput, calls=%fused_computation.3.clone.1.clone | convolution fusion | flops 25985024 | bytes 3427585 | tf_op jit(solution)/shard_map/jvp()/while/body/eval_jaxpr/skh,skhp,skn->khpn/dot_general | solution.py:40
  148.5 7.4 %bitcast_dynamic-update-slice_fusion.22 = (f32[4,8,4,16,64]{4,1,3,2,0:T(8,128)}, f32[4,8,16,64]{3,1,2,0:T(8,128)}) fusion(f32[4,8,4,16,64]{4,1,3,2,0:T(8,128)} %get-tuple-element.2468, s32[]{:T(128)} %get-tuple-element.2457, f32[4,16,64,64]{3,2,1,0:T(8,128)} %get-tuple-element.2458, pred[]{:T(512)S(6)} %compare.11, ...), kind=kOutput, calls=%fused_computation.13.clone.1.clone | convolution fusion | flops 25427968 | bytes 2638849 | tf_op jit(solution)/shard_map/jvp()/while/body/eval_jaxpr/tkn,khpn->tkhp/dot_general | solution.py:34
  155.8 3.2 bitcast_dynamic-update-slice_fusion.25
  159.1 6.9 %multiply_add_fusion.7 = f32[4,16,64,64]{3,2,1,0:T(8,128)} fusion(f32[4,16,64,64]{3,2,1,0:T(8,128)} %get-tuple-element.2458, f32[4,16]{1,0:T(4,128)S(1)} %negate_exponential_fusion.8, pred[]{:T(512)S(6)} %compare.11, f32[4,8,4,16,64]{4,1,3,2,0:T(8,128)} %get-tuple-element.2502, s32[]{:T(128)} %get-tuple-element.2457, ...), kind=kOutput, calls=%fused_computation.3.clone.1.clone | convolution fusion | flops 25985024 | bytes 3427585 | tf_op jit(solution)/shard_map/jvp()/while/body/eval_jaxpr/skh,skhp,skn->khpn/dot_general | solution.py:40
  177.4 8.7 %all_to_all.24 = bf16[32,4,1024]{2,1,0:T(4,128)(2,1)S(1)} all-to-all(bf16[32,4,1024]{2,1,0:T(4,128)(2,1)S(1)} %reshape.394), channel_id=1, replica_groups=mesh['tm'=4,'space'=8] {'tm'}, dimensions={0} | all-to-all | bytes 524288 | tf_op jit(solution)/shard_map/all_to_all | solution.py:176
  195.3 3.6 all-to-all-start.3
  199.5 4.5 all-to-all-done.3
  208.4 216.1 %while.78 = (s32[]{:T(128)}, f32[16]{0:T(128)}, f32[16]{0:T(128)}, f32[4,16,64,64]{3,2,1,0:T(8,128)}, bf16[4,8,4,16,64]{4,1,3,2,0:T(8,128)(2,1)}, /*index=5*/bf1...) while((s32[]{:T(128)}, f32[16]{0:T(128)}, f32[16]{0:T(128)}, ...), condition=%wide.region_16.17_spmd.clone.clone.clone, body=%wide.region_5.16_spmd.clone.clone.sunk.clone | while | flops 109901728 | bytes 16311662 | solution.py:60
  209.4 7.4 %fusion.276 = (f32[16]{0:T(128)}, f32[8,4,16]{0,2,1:T(8,128)}, f32[8,4,16]{0,2,1:T(8,128)}, f32[8,4,16,64]{3,0,2,1:T(8,128)}) fusion(f32[4,8,4,16,64]{4,1,3,2,0:T(8,128)} %get-tuple-element.2579, s32[]{:T(128)S(6)} %sub.208, f32[1,8,4,16,64]{4,3,1,2,0:T(8,128)S(1)} %constant_dynamic-slice_fusion.17, ...), kind=kOutput, calls=%fused_computation.125.clone.1.clone | convolution fusion | flops 25623536 | bytes 2905664 | tf_op jit(solution)/shard_map/transpose(jvp())/while/body/eval_jaxpr/skh,skhp,skn->khpn/dot_general | solution.py:40
  227.1 2.7 fusion.275
  248.2 5.8 multiply_add_fusion.8
  254.6 2.9 fusion.286
  261.5 8.0 %fusion.276 = (f32[16]{0:T(128)}, f32[8,4,16]{0,2,1:T(8,128)}, f32[8,4,16]{0,2,1:T(8,128)}, f32[8,4,16,64]{3,0,2,1:T(8,128)}) fusion(f32[4,8,4,16,64]{4,1,3,2,0:T(8,128)} %get-tuple-element.2579, s32[]{:T(128)S(6)} %sub.208, f32[1,8,4,16,64]{4,3,1,2,0:T(8,128)S(1)} %constant_dynamic-slice_fusion.17, ...), kind=kOutput, calls=%fused_computation.125.clone.1.clone | convolution fusion | flops 25623536 | bytes 2905664 | tf_op jit(solution)/shard_map/transpose(jvp())/while/body/eval_jaxpr/skh,skhp,skn->khpn/dot_general | solution.py:40
  296.1 2.9 fusion.284
  302.4 6.2 multiply_add_fusion.8
  309.2 2.9 fusion.286
  316.2 8.0 %fusion.276 = (f32[16]{0:T(128)}, f32[8,4,16]{0,2,1:T(8,128)}, f32[8,4,16]{0,2,1:T(8,128)}, f32[8,4,16,64]{3,0,2,1:T(8,128)}) fusion(f32[4,8,4,16,64]{4,1,3,2,0:T(8,128)} %get-tuple-element.2579, s32[]{:T(128)S(6)} %sub.208, f32[1,8,4,16,64]{4,3,1,2,0:T(8,128)S(1)} %constant_dynamic-slice_fusion.17, ...), kind=kOutput, calls=%fused_computation.125.clone.1.clone | convolution fusion | flops 25623536 | bytes 2905664 | tf_op jit(solution)/shard_map/transpose(jvp())/while/body/eval_jaxpr/skh,skhp,skn->khpn/dot_general | solution.py:40
  350.7 2.9 fusion.284
  357.0 6.2 multiply_add_fusion.8
  363.9 2.9 fusion.286
  370.8 8.0 %fusion.276 = (f32[16]{0:T(128)}, f32[8,4,16]{0,2,1:T(8,128)}, f32[8,4,16]{0,2,1:T(8,128)}, f32[8,4,16,64]{3,0,2,1:T(8,128)}) fusion(f32[4,8,4,16,64]{4,1,3,2,0:T(8,128)} %get-tuple-element.2579, s32[]{:T(128)S(6)} %sub.208, f32[1,8,4,16,64]{4,3,1,2,0:T(8,128)S(1)} %constant_dynamic-slice_fusion.17, ...), kind=kOutput, calls=%fused_computation.125.clone.1.clone | convolution fusion | flops 25623536 | bytes 2905664 | tf_op jit(solution)/shard_map/transpose(jvp())/while/body/eval_jaxpr/skh,skhp,skn->khpn/dot_general | solution.py:40
  389.8 2.7 fusion.275
  405.4 2.9 fusion.284
  411.7 6.2 multiply_add_fusion.8
  418.5 2.9 fusion.286
  425.9 3.2 all-to-all-start.5
  429.2 3.9 convolution_bitcast_fusion.4
  439.0 4.2 all-to-all-start.4
  443.7 4.9 all-to-all-done.4
  453.5 4.2 collective-permute-done.3
  461.0 5.9 pad_maximum_fusion
  466.9 13.9 %copy.282 = f32[1024,3216]{1,0:T(8,128)} copy(f32[1024,3216]{0,1:T(8,128)} %pad_maximum_fusion) | data formatting | bytes 26345472
  483.4 46.3 %all-reduce.3 = (f32[3,3,1152]{2,1,0:T(4,128)}, f32[1152]{0:T(1024)}, f32[16]{0:T(128)}, f32[16]{0:T(128)}, f32[16]{0:T(128)}, /*index=5*/f32[1024]{0:T(1024)}) all-reduce(f32[3,3,1152]{2,1,0:T(4,128)S(1)} %reshape.370, f32[1152]{0:T(1024)S(1)} %get-tuple-element.1697, ...), channel_id=1, replica_groups=mesh['tm'=4,'space'=8] {'tm','space'}, use_global_device_ids=true, to_apply=%region_27.28 | all-reduce | flops 12592 | bytes 100736 | tf_op jit(solution)/shard_map/psum | solution.py:266
  529.7 3.9 fusion.174
  534.5 116.4 %reduce-scatter.4.cloned.1.call-done = f32[32,3216]{1,0:T(8,128)} async-done(((f32[1024,3216]{1,0:T(8,128)}), f32[32,3216]{1,0:T(8,128)}) %reduce-scatter.4.cloned.1.call-update) | async-done | bytes 411664
  (446 shorter events, 255.0 us)
Async XLA Ops:
  7.2 183.6 %copy-start = (bf16[1024,1024]{1,0:T(8,128)(2,1)S(1)}, bf16[1024,1024]{1,0:T(8,128)(2,1)}, u32[]{:S(2)}) copy-start(bf16[1024,1024]{1,0:T(8,128)(2,1)} %param.24) | copy-start | bytes 6291460
  7.2 8.7 %copy-start.11 = (bf16[8,2,8,1024]{3,2,1,0:T(8,128)(2,1)S(1)}, bf16[8,2,8,1024]{3,2,1,0:T(8,128)(2,1)}, u32[]{:S(2)}) copy-start(bf16[8,2,8,1024]{3,2,1,0:T(8,128)(2,1)} %param.15) | copy-start | bytes 786436
  7.2 8.7 %copy-start.43 = (bf16[1024,16]{0,1:T(8,128)(2,1)S(1)}, bf16[1024,16]{0,1:T(8,128)(2,1)}, u32[]{:S(2)}) copy-start(bf16[1024,16]{0,1:T(8,128)(2,1)} %param.17) | copy-start | bytes 98308
  7.2 8.7 %copy-start.58 = (f32[16]{0:T(128)S(1)}, f32[16]{0:T(128)}, u32[]{:S(2)}) copy-start(f32[16]{0:T(128)} %param.18) | copy-start | bytes 196
  11.3 10.9 %copy-start.45 = (f32[3,3,1152]{2,1,0:T(4,128)S(1)}, f32[3,3,1152]{2,1,0:T(4,128)}, u32[]{:S(2)}) copy-start(f32[3,3,1152]{2,1,0:T(4,128)} %param.20) | copy-start | bytes 124420
  12.2 15.9 %copy-start.54 = (f32[1152]{0:T(1024)S(1)}, f32[1152]{0:T(1024)}, u32[]{:S(2)}) copy-start(f32[1152]{0:T(1024)} %param.21) | copy-start | bytes 13828
  12.2 14.7 %collective-permute-start = (bf16[8,1,8,1152]{3,0,2,1:T(8,128)(2,1)S(1)}, bf16[8,1,8,1152]{3,0,2,1:T(8,128)(2,1)S(1)}, u32[]{:S(2)}, u32[]{:S(2)}) collective-permute-start(bf16[8,1,8,1152]{3,0,2,1:T(8,128)(2,1)S(1)} %get-tuple-element.1864), channel_id=1, source_target_pairs={{0,1},{1,2},{2,3},{3,4},{4,5},{5,6},{6,7},{8,9},{9,10},{10,11},{11... | collective-permute-start | bytes 442376 | tf_op jit(solution)/shard_map/ppermute | solution.py:15
  14.6 12.3 %collective-permute-start.1 = (bf16[8,1,8,1152]{3,0,2,1:T(8,128)(2,1)S(1)}, bf16[8,1,8,1152]{3,0,2,1:T(8,128)(2,1)}, u32[]{:S(2)}, u32[]{:S(2)}) collective-permute-start(bf16[8,1,8,1152]{3,0,2,1:T(8,128)(2,1)S(1)} %get-tuple-element.1865), channel_id=1, source_target_pairs={{1,0},{2,1},{3,2},{4,3},{5,4},{6,5},{7,6},{9,8},{10,9},{11,10},{12... | collective-permute-start | bytes 442376 | tf_op jit(solution)/shard_map/ppermute | solution.py:18
  17.6 9.2 %all-to-all-start = ((bf16[4,2,256]{2,1,0:T(2,128)(2,1)}), bf16[4,2,256]{2,1,0:T(2,128)(2,1)S(1)}, u32[]{:S(2)}, u32[]{:S(2)}) async-start(bf16[4,2,256]{2,1,0:T(2,128)(2,1)} %reshape.406), calls=%async_computation | async-start | bytes 8192 | tf_op jit(solution)/shard_map/all_to_all | solution.py:158
  22.4 7.1 %copy-start.20 = (f32[1152]{0:T(1024)}, f32[1152]{0:T(1024)S(1)}, u32[]{:S(2)}) copy-start(f32[1152]{0:T(1024)S(1)} %get-tuple-element.1698) | copy-start | bytes 13828
  22.4 7.1 %copy-start.22 = (f32[1152]{0:T(1024)}, f32[1152]{0:T(1024)S(1)}, u32[]{:S(2)}) copy-start(f32[1152]{0:T(1024)S(1)} %get-tuple-element.1699) | copy-start | bytes 13828
  22.4 7.1 %copy-start.24 = (f32[1152]{0:T(1024)}, f32[1152]{0:T(1024)S(1)}, u32[]{:S(2)}) copy-start(f32[1152]{0:T(1024)S(1)} %get-tuple-element.1700) | copy-start | bytes 13828
  22.4 7.1 %copy-start.26 = (f32[1152]{0:T(1024)}, f32[1152]{0:T(1024)S(1)}, u32[]{:S(2)}) copy-start(f32[1152]{0:T(1024)S(1)} %get-tuple-element.1701) | copy-start | bytes 13828
  22.4 7.1 %copy-start.28 = (f32[1152]{0:T(1024)}, f32[1152]{0:T(1024)S(1)}, u32[]{:S(2)}) copy-start(f32[1152]{0:T(1024)S(1)} %get-tuple-element.1702) | copy-start | bytes 13828
  22.4 7.1 %copy-start.30 = (f32[1152]{0:T(1024)}, f32[1152]{0:T(1024)S(1)}, u32[]{:S(2)}) copy-start(f32[1152]{0:T(1024)S(1)} %get-tuple-element.1703) | copy-start | bytes 13828
  22.4 7.1 %copy-start.32 = (f32[1152]{0:T(1024)}, f32[1152]{0:T(1024)S(1)}, u32[]{:S(2)}) copy-start(f32[1152]{0:T(1024)S(1)} %get-tuple-element.1704) | copy-start | bytes 13828
  22.4 7.1 %copy-start.34 = (f32[1152]{0:T(1024)}, f32[1152]{0:T(1024)S(1)}, u32[]{:S(2)}) copy-start(f32[1152]{0:T(1024)S(1)} %get-tuple-element.1705) | copy-start | bytes 13828
  22.5 7.1 %copy-start.36 = (f32[1152]{0:T(1024)}, f32[1152]{0:T(1024)S(1)}, u32[]{:S(2)}) copy-start(f32[1152]{0:T(1024)S(1)} %get-tuple-element.1706) | copy-start | bytes 13828
  29.6 11.1 %all-to-all-start.1 = ((bf16[8,16,1152]{2,0,1:T(8,128)(2,1)}), bf16[8,16,1152]{2,0,1:T(8,128)(2,1)}, u32[]{:S(2)}, u32[]{:S(2)}) async-start(bf16[8,16,1152]{2,0,1:T(8,128)(2,1)} %bitcast.603), calls=%async_computation.1 | async-start | bytes 589824 | tf_op jit(solution)/shard_map/all_to_all | solution.py:157
  43.8 7.3 %copy-start.40 = (f32[16]{0:T(128)S(1)}, f32[16]{0:T(128)}, u32[]{:S(2)}) copy-start(f32[16]{0:T(128)} %param.19) | copy-start | bytes 196
  43.8 7.3 %copy-start.53 = (f32[16]{0:T(128)S(1)}, f32[16]{0:T(128)}, u32[]{:S(2)}) copy-start(f32[16]{0:T(128)} %param.22) | copy-start | bytes 196
  195.3 8.8 %all-to-all-start.3 = ((bf16[8,16,1024]{2,0,1:T(8,128)(2,1)}), bf16[8,16,1024]{2,0,1:T(8,128)(2,1)S(1)}, u32[]{:S(2)}, u32[]{:S(2)}) async-start(bf16[8,16,1024]{2,0,1:T(8,128)(2,1)} %copy.246), calls=%async_computation.3 | async-start | bytes 524288 | tf_op jit(solution)/shard_map/all_to_all | solution.py:201
  248.2 6.4 copy-start.4
  302.4 6.3 copy-start.42
  302.4 6.3 copy-start.46
  302.4 6.3 copy-start.49
  302.4 6.8 %copy-start.4 = (f32[1,8,4,16,1]{1,3,2,4,0:T(8,128)S(1)}, f32[1,8,4,16,1]{1,3,2,4,0:T(8,128)}, u32[]{:S(2)}) copy-start(f32[1,8,4,16,1]{1,3,2,4,0:T(8,128)} %copy.392) | copy-start | bytes 6148 | tf_op jit(solution)/shard_map/transpose(jvp())/while
  357.0 6.3 copy-start.46
  357.0 6.3 copy-start.49
  357.0 6.8 %copy-start.4 = (f32[1,8,4,16,1]{1,3,2,4,0:T(8,128)S(1)}, f32[1,8,4,16,1]{1,3,2,4,0:T(8,128)}, u32[]{:S(2)}) copy-start(f32[1,8,4,16,1]{1,3,2,4,0:T(8,128)} %copy.392) | copy-start | bytes 6148 | tf_op jit(solution)/shard_map/transpose(jvp())/while
  411.7 6.3 copy-start.46
  411.7 6.3 copy-start.49
  411.7 6.8 %copy-start.4 = (f32[1,8,4,16,1]{1,3,2,4,0:T(8,128)S(1)}, f32[1,8,4,16,1]{1,3,2,4,0:T(8,128)}, u32[]{:S(2)}) copy-start(f32[1,8,4,16,1]{1,3,2,4,0:T(8,128)} %copy.392) | copy-start | bytes 6148 | tf_op jit(solution)/shard_map/transpose(jvp())/while
  425.9 13.0 %all-to-all-start.5 = ((bf16[4,2,256]{2,1,0:T(2,128)(2,1)}), bf16[4,2,256]{2,1,0:T(2,128)(2,1)S(1)}, u32[]{:S(2)}, u32[]{:S(2)}) async-start(bf16[4,2,256]{2,1,0:T(2,128)(2,1)} %reshape.408), calls=%async_computation.5 | async-start | bytes 8192 | tf_op jit(solution)/shard_map/all_to_all | solution.py:216
  433.1 10.4 %copy-start.57 = (f32[128,16]{0,1:T(8,128)S(1)}, f32[128,16]{0,1:T(8,128)}, u32[]{:S(2)}) copy-start(f32[128,16]{0,1:T(8,128)} %get-tuple-element.1867) | copy-start | bytes 24580
  439.0 9.7 %all-to-all-start.4 = ((bf16[32,4,1152]{2,1,0:T(4,128)(2,1)}), bf16[32,4,1152]{2,1,0:T(4,128)(2,1)}, u32[]{:S(2)}, u32[]{:S(2)}) async-start(bf16[32,4,1152]{2,1,0:T(4,128)(2,1)} %copy.260), calls=%async_computation.4 | async-start | bytes 589824 | tf_op jit(solution)/shard_map/all_to_all | solution.py:215
  443.1 207.8 %reduce-scatter.4.cloned.1.call-start = ((), (), s32[]{:S(2)}) async-start(), calls=%async_computation.7 | async-start | bytes 14057472
  450.5 7.3 %copy-start.21 = (f32[1152]{0:T(1024)S(1)}, f32[1152]{0:T(1024)}, u32[]{:S(2)}) copy-start(f32[1152]{0:T(1024)} %copy-done.20) | copy-start | bytes 13828
  450.5 7.3 %copy-start.23 = (f32[1152]{0:T(1024)S(1)}, f32[1152]{0:T(1024)}, u32[]{:S(2)}) copy-start(f32[1152]{0:T(1024)} %copy-done.22) | copy-start | bytes 13828
  450.5 7.3 %copy-start.25 = (f32[1152]{0:T(1024)S(1)}, f32[1152]{0:T(1024)}, u32[]{:S(2)}) copy-start(f32[1152]{0:T(1024)} %copy-done.24) | copy-start | bytes 13828
  450.5 7.3 %copy-start.27 = (f32[1152]{0:T(1024)S(1)}, f32[1152]{0:T(1024)}, u32[]{:S(2)}) copy-start(f32[1152]{0:T(1024)} %copy-done.26) | copy-start | bytes 13828
  450.5 7.3 %copy-start.29 = (f32[1152]{0:T(1024)S(1)}, f32[1152]{0:T(1024)}, u32[]{:S(2)}) copy-start(f32[1152]{0:T(1024)} %copy-done.28) | copy-start | bytes 13828
  450.5 7.3 %copy-start.31 = (f32[1152]{0:T(1024)S(1)}, f32[1152]{0:T(1024)}, u32[]{:S(2)}) copy-start(f32[1152]{0:T(1024)} %copy-done.30) | copy-start | bytes 13828
  450.5 7.3 %copy-start.33 = (f32[1152]{0:T(1024)S(1)}, f32[1152]{0:T(1024)}, u32[]{:S(2)}) copy-start(f32[1152]{0:T(1024)} %copy-done.32) | copy-start | bytes 13828
  450.6 7.3 %copy-start.35 = (f32[1152]{0:T(1024)S(1)}, f32[1152]{0:T(1024)}, u32[]{:S(2)}) copy-start(f32[1152]{0:T(1024)} %copy-done.34) | copy-start | bytes 13828
  450.6 7.3 %copy-start.37 = (f32[1152]{0:T(1024)S(1)}, f32[1152]{0:T(1024)}, u32[]{:S(2)}) copy-start(f32[1152]{0:T(1024)} %copy-done.36) | copy-start | bytes 13828
  450.6 2.9 collective-permute-start.2
  452.0 5.7 collective-permute-start.3
  (51 other events, 139.3 us)
Sparse Core Ops, SparseCore 0:
  481.0 169.8 reduce-scatter.3
where the time goes:
time: 672 us; the launch traced here: 662 us
  matrix products  197 us (29%)
  waiting for transfers between devices  140 us (21%)
  local copies, waits for them, and re-layouts  139 us (21%)
  other arithmetic  90.1 us (13%)
  blocking collectives  55 us (8%)
  starting transfers between devices  26.5 us (4%)
  between operations  15 us (2%)
    unnamed x2, waiting for transfers between devices  116 us
    dot_general x12, matrix products, ssd_block(): jnp.einsum('skh,skhp,skn->khpn', tail_weight, heads_in, b_proj, precision...  68.9 us
    dot_general x12, matrix products, ssd_block(): jnp.einsum('tkn,khpn->tkhp', c_proj, state_in, precision=top_precision)  64.8 us
    psum x1, blocking collectives, on_device(): lax.psum((kernel_part, conv_bias_part, bias_part, rate_part, gain_part, n...  46.3 us
    dynamic_slice x32, local copies, waits for them, and re-layouts, ssd_sequence(): lax.scan(advance, start_state, (fold_blocks(heads_in), fold_blocks(b_proj...  42 us
    dynamic_update_slice x28, other arithmetic, ssd_sequence(): lax.scan(advance, start_state, (fold_blocks(heads_in), fold_blocks(b_proj...  38.8 us
    dot_general x12, matrix products, ssd_block(): jnp.einsum('tskh,skhp->tkhp', weights * inner_cb[..., None], heads_in, pr...  30.2 us
    unnamed x109, local copies, waits for them, and re-layouts  27 us
  transfers between devices with their start and end apart: 10, of which 6 were waited for; matrix products, arithmetic and copies ran while one was open for 3% of the time, Pallas kernels for 0%

commit v1 on v0

v1 whole, which is shorter than its diff:
```python
import functools

import jax
import jax.numpy as jnp
from jax import lax
from jax.experimental import pallas as pl
from jax.experimental.pallas import tpu as pltpu
from jax.sharding import PartitionSpec as P

top_precision = lax.Precision.HIGHEST
norm_eps = 1e-05
LANES = 128
VMEM_BYTES = 40 * 1024 * 1024

contract_rows = (((0,), (0,)), ((), ()))
contract_cols = (((1,), (1,)), ((), ()))


def dot_f32(left, right, dims=(((1,), (0,)), ((), ()))):
    return lax.dot_general(left, right, dims, preferred_element_type=jnp.float32)


def half(value):
    return value.astype(jnp.bfloat16)


def whole_call(body, out_shape, scratch=()):
    return pl.pallas_call(
        body,
        out_shape=out_shape,
        scratch_shapes=scratch,
        compiler_params=pltpu.CompilerParams(vmem_limit_bytes=VMEM_BYTES),
    )


def ssd_kernel(
    few,
    act_ref,
    gate_ref,
    d_normed_ref,
    run_ref,
    run_t_ref,
    step_t_ref,
    skip_ref,
    norm_gain_ref,
    normed_ref,
    d_gate_ref,
    d_act_ref,
    row_ref,
    col_ref,
    skip_part_ref,
    norm_part_ref,
    decay_ref,
    ssd_ref,
    d_ssd_ref,
):
    count = act_ref.shape[0]
    inner_w = gate_ref.shape[1]
    heads = run_ref.shape[1]
    head_dim = inner_w // heads
    per_tile = LANES // head_dim
    rows = lax.broadcasted_iota(jnp.int32, (count, count), 0)
    cols = lax.broadcasted_iota(jnp.int32, (count, count), 1)
    causal = (lax.rem(rows, few) == lax.rem(cols, few)) & (rows >= cols)
    lane = lax.broadcasted_iota(jnp.int32, (count, LANES), 1)
    low = lane < head_dim
    bc = act_ref[:, inner_w:]
    swapped_float = pltpu.roll(bc.astype(jnp.float32), head_dim, 1)
    swapped = half(swapped_float)
    inner_cb = dot_f32(half(jnp.where(low, swapped_float, 0.0)), bc, contract_cols)
    inner_cb = jnp.where(causal, inner_cb, 0.0)

    for tile in range(inner_w // LANES):
        span = slice(tile * LANES, (tile + 1) * LANES)
        u = act_ref[:, span]
        result = u.astype(jnp.float32) * skip_ref[:, span]
        for place in range(per_tile):
            h = tile * per_tile + place
            spread = run_t_ref[h : h + 1, :] - run_ref[:, h : h + 1]
            decay = jnp.exp(jnp.where(causal, spread, 0.0))
            decay_ref[h] = decay
            weights = half(inner_cb * decay * step_t_ref[h : h + 1, :])
            mine = lane // head_dim == place
            result = result + jnp.where(mine, dot_f32(weights, u), 0.0)
        ssd_ref[:, span] = half(result)

    squares = jnp.zeros((count, LANES), jnp.float32)
    crossed = jnp.zeros((count, LANES), jnp.float32)
    for tile in range(inner_w // LANES):
        span = slice(tile * LANES, (tile + 1) * LANES)
        gate = gate_ref[:, span].astype(jnp.float32)
        gated = ssd_ref[:, span].astype(jnp.float32) * (gate * jax.nn.sigmoid(gate))
        squares = squares + gated * gated
        crossed = crossed + gated * (d_normed_ref[:, span] * norm_gain_ref[:, span])
    mean_square = jnp.sum(squares, axis=1, keepdims=True) / inner_w
    scale_row = lax.rsqrt(mean_square + norm_eps)
    pulled = jnp.sum(crossed, axis=1, keepdims=True) / inner_w * scale_row * scale_row
    for tile in range(inner_w // LANES):
        span = slice(tile * LANES, (tile + 1) * LANES)
        gate = gate_ref[:, span].astype(jnp.float32)
        squashed = jax.nn.sigmoid(gate)
        silu = gate * squashed
        ssd = ssd_ref[:, span].astype(jnp.float32)
        gated = ssd * silu
        scaled = gated * scale_row
        d_normed = d_normed_ref[:, span]
        normed_ref[:, span] = half(scaled * norm_gain_ref[:, span])
        norm_part_ref[:, span] = jnp.sum(d_normed * scaled, axis=0, keepdims=True)
        d_gated = scale_row * (d_normed * norm_gain_ref[:, span] - gated * pulled)
        d_ssd_ref[:, span] = half(d_gated * silu)
        d_gate_ref[:, span] = half(d_gated * ssd * (squashed * (1.0 + gate * (1.0 - squashed))))

    d_cb = jnp.zeros((count, count), jnp.float32)
    for tile in range(inner_w // LANES):
        span = slice(tile * LANES, (tile + 1) * LANES)
        u = act_ref[:, span]
        d_y = d_ssd_ref[:, span]
        d_y_float = d_y.astype(jnp.float32)
        d_u = d_y_float * skip_ref[:, span]
        skip_part_ref[:, span] = jnp.sum(d_y_float * u.astype(jnp.float32), axis=0, keepdims=True)
        for place in range(per_tile):
            h = tile * per_tile + place
            mine = lane // head_dim == place
            d_weights = dot_f32(half(jnp.where(mine, d_y_float, 0.0)), u, contract_cols)
            decay = decay_ref[h]
            step_row = step_t_ref[h : h + 1, :]
            d_scaled = d_weights * decay
            d_cb = d_cb + d_scaled * step_row
            product = d_scaled * inner_cb
            col_ref[h : h + 1, :] = jnp.sum(product, axis=0, keepdims=True)
            row_ref[:, h : h + 1] = jnp.sum(product * step_row, axis=1, keepdims=True)
            weights = half(inner_cb * decay * step_row)
            d_u = d_u + jnp.where(mine, dot_f32(weights, d_y, contract_rows), 0.0)
        d_act_ref[:, span] = half(d_u)
    d_cb = half(jnp.where(causal, d_cb, 0.0))
    d_act_ref[:, inner_w:] = half(
        jnp.where(low, dot_f32(d_cb, swapped, contract_rows), dot_f32(d_cb, swapped))
    )


def sideways(flat, cols):
    rows = flat.shape[0]
    col = lax.rem(lax.broadcasted_iota(jnp.int32, flat.shape, 0), cols)
    left = jnp.where(col > 0, pltpu.roll(flat, 1, 0), 0.0)
    right = jnp.where(col < cols - 1, pltpu.roll(flat, rows - 1, 0), 0.0)
    return left, flat, right


def tall_tile(low_ref, mid_ref, high_ref, span):
    stacked = jnp.concatenate(
        [ref[:, :, :, span].astype(jnp.float32) for ref in (low_ref, mid_ref, high_ref)], axis=1
    )
    return stacked, stacked.reshape(-1, stacked.shape[-1])


def conv_kernel_body(low_ref, mid_ref, high_ref, kernel_ref, bias_ref, before_ref, act_ref):
    row_count, cols = mid_ref.shape[1], mid_ref.shape[2]
    for tile in range(mid_ref.shape[3] // LANES):
        span = slice(tile * LANES, (tile + 1) * LANES)
        stacked, flat = tall_tile(low_ref, mid_ref, high_ref, span)
        total = bias_ref[:, span].reshape(1, 1, 1, -1)
        for col_off, moved in enumerate(sideways(flat, cols)):
            moved = moved.reshape(stacked.shape)
            for row_off in range(3):
                k = 3 * row_off + col_off
                tap = kernel_ref[k : k + 1, span].reshape(1, 1, 1, -1)
                total = total + tap * moved[:, row_off : row_off + row_count]
        before_ref[:, :, :, span] = total
        act_ref[:, :, :, span] = half(total * jax.nn.sigmoid(total))


def d_before_body(d_act_ref, before_ref, d_before_ref, d_half_ref):
    for tile in range(before_ref.shape[3] // LANES):
        span = slice(tile * LANES, (tile + 1) * LANES)
        before = before_ref[:, :, :, span]
        squashed = jax.nn.sigmoid(before)
        slope = squashed * (1.0 + before * (1.0 - squashed))
        d_before = d_act_ref[:, :, :, span].astype(jnp.float32) * slope
        d_before_ref[:, :, :, span] = d_before
        d_half_ref[:, :, :, span] = half(d_before)


def kernel_grad_body(low_ref, mid_ref, high_ref, d_before_ref, part_ref):
    row_count, cols = mid_ref.shape[1], mid_ref.shape[2]
    for tile in range(mid_ref.shape[3] // LANES):
        span = slice(tile * LANES, (tile + 1) * LANES)
        stacked, flat = tall_tile(low_ref, mid_ref, high_ref, span)
        d_before = d_before_ref[:, :, :, span]
        for col_off, moved in enumerate(sideways(flat, cols)):
            moved = moved.reshape(stacked.shape)
            for row_off in range(3):
                product = d_before * moved[:, row_off : row_off + row_count]
                k = 3 * row_off + col_off
                part_ref[k : k + 1, span] = jnp.sum(
                    product.reshape(-1, LANES), axis=0, keepdims=True
                )
        part_ref[9:10, span] = jnp.sum(d_before.reshape(-1, LANES), axis=0, keepdims=True)


def d_mixed_body(low_ref, mid_ref, high_ref, kernel_ref, d_mixed_ref):
    row_count, cols = mid_ref.shape[1], mid_ref.shape[2]
    for tile in range(mid_ref.shape[3] // LANES):
        span = slice(tile * LANES, (tile + 1) * LANES)
        stacked, flat = tall_tile(low_ref, mid_ref, high_ref, span)
        total = jnp.zeros(mid_ref.shape[:3] + (LANES,), jnp.float32)
        for shift, moved in enumerate(sideways(flat, cols)):
            moved = moved.reshape(stacked.shape)
            for row_off in range(3):
                k = 3 * row_off + 2 - shift
                tap = kernel_ref[k : k + 1, span].reshape(1, 1, 1, -1)
                total = total + tap * moved[:, 2 - row_off : 2 - row_off + row_count]
        d_mixed_ref[:, :, :, span] = half(total)


def edges(block):
    count = lax.axis_size("space")
    forward = [(i, i + 1) for i in range(count - 1)]
    backward = [(i + 1, i) for i in range(count - 1)]
    low = lax.ppermute(block[:, -1:], "space", forward)
    high = lax.ppermute(block[:, :1], "space", backward)
    return low, high


def to_sequences(block):
    parts = lax.axis_size("tm")
    frames, tokens, width = block.shape
    few = tokens // parts
    sent = block.reshape(frames, parts, few, width).transpose(1, 0, 2, 3)
    sent = sent.reshape(parts, frames * few, width)
    got = lax.all_to_all(sent, "tm", split_axis=0, concat_axis=0, tiled=True)
    return got.reshape(parts * frames * few, width)


def to_frames(flat, frames):
    parts = lax.axis_size("tm")
    few = flat.shape[0] // (parts * frames)
    width = flat.shape[1]
    got = lax.all_to_all(
        flat.reshape(parts, frames * few, width), "tm", split_axis=0, concat_axis=0, tiled=True
    )
    got = got.reshape(parts, frames, few, width).transpose(1, 0, 2, 3)
    return got.reshape(frames, parts * few, width)


def scatter_sum(partial):
    return lax.psum_scatter(
        half(partial), ("tm", "space"), scatter_dimension=0, tiled=True
    ).astype(jnp.float32)


def on_device(
    activations,
    in_proj,
    step_proj,
    step_bias,
    decay_rates,
    conv_kernel,
    conv_bias,
    skip_gain,
    norm_gain,
    out_proj,
    out_cotangent,
):
    frame_count, row_count, col_count, model_width = activations.shape
    inner_w = out_proj.shape[0]
    head_count = step_proj.shape[1]
    head_dim = inner_w // head_count
    conv_w = in_proj.shape[1] - inner_w
    token_count = row_count * col_count
    few = token_count // lax.axis_size("tm")
    grid = (frame_count, row_count, col_count)

    flat_act = activations.reshape(-1, model_width)
    mixed_in = half(dot_f32(flat_act, in_proj[:, inner_w:])).reshape(grid + (conv_w,))
    low, high = edges(mixed_in)
    both = jnp.concatenate([activations, out_cotangent], axis=-1)
    both_seq = to_sequences(both.reshape(frame_count, token_count, -1))
    flat_kernel = conv_kernel.reshape(9, conv_w)
    before, activated = whole_call(
        conv_kernel_body,
        (
            jax.ShapeDtypeStruct(grid + (conv_w,), jnp.float32),
            jax.ShapeDtypeStruct(grid + (conv_w,), jnp.bfloat16),
        ),
    )(low, mixed_in, high, flat_kernel, conv_bias.reshape(1, -1))
    act_seq = to_sequences(activated.reshape(frame_count, token_count, conv_w))

    x_seq, cot_seq = both_seq[:, :model_width], both_seq[:, model_width:]
    count = x_seq.shape[0]
    gate_z = half(dot_f32(x_seq, in_proj[:, :inner_w]))
    step_raw = dot_f32(x_seq, step_proj) + step_bias
    steps = half(jax.nn.softplus(step_raw)).astype(jnp.float32)
    d_normed = dot_f32(cot_seq, out_proj, contract_cols)
    index = jnp.arange(count)
    earlier = (
        (index[:, None] % few == index[None, :] % few) & (index[:, None] >= index[None, :])
    ).astype(jnp.float32)
    running = jnp.dot(earlier, steps * decay_rates, precision=top_precision)
    f32, bf16 = jnp.float32, jnp.bfloat16
    normed, d_gate, d_act_seq, row_sums, col_sums, skip_part, norm_part = whole_call(
        functools.partial(ssd_kernel, few),
        (
            jax.ShapeDtypeStruct((count, inner_w), bf16),
            jax.ShapeDtypeStruct((count, inner_w), bf16),
            jax.ShapeDtypeStruct((count, conv_w), bf16),
            jax.ShapeDtypeStruct((count, head_count), f32),
            jax.ShapeDtypeStruct((head_count, count), f32),
            jax.ShapeDtypeStruct((1, inner_w), f32),
            jax.ShapeDtypeStruct((1, inner_w), f32),
        ),
        (
            pltpu.VMEM((head_count, count, count), f32),
            pltpu.VMEM((count, inner_w), bf16),
            pltpu.VMEM((count, inner_w), bf16),
        ),
    )(
        act_seq,
        gate_z,
        d_normed,
        running,
        running.T,
        steps.T,
        jnp.repeat(skip_gain, head_dim).reshape(1, -1),
        norm_gain.reshape(1, -1),
    )
    d_act = to_frames(d_act_seq, frame_count).reshape(grid + (conv_w,))
    layer_seq = half(dot_f32(normed, out_proj))
    col_turned = col_sums.T
    d_running = col_turned * steps - row_sums
    d_decay = jnp.dot(earlier.T, d_running, precision=top_precision)
    d_steps = half(col_turned + d_decay * decay_rates).astype(f32)
    rate_part = jnp.sum(d_decay * steps, axis=0)
    gain_part = jnp.sum(skip_part.reshape(head_count, head_dim), axis=1)
    d_raw = d_steps * jax.nn.sigmoid(step_raw)
    bias_part = jnp.sum(d_raw, axis=0)
    d_raw_half = half(d_raw)
    back = to_frames(jnp.concatenate([d_gate, layer_seq, d_raw_half], axis=1), frame_count)
    back = back.reshape(-1, back.shape[-1])
    early = scatter_sum(
        jnp.concatenate(
            [
                dot_f32(x_seq, d_gate, contract_rows),
                dot_f32(cot_seq, normed, contract_rows),
                dot_f32(x_seq, d_raw_half, contract_rows),
            ],
            axis=1,
        )
    )

    d_before, d_half = whole_call(
        d_before_body,
        (
            jax.ShapeDtypeStruct(before.shape, f32),
            jax.ShapeDtypeStruct(before.shape, bf16),
        ),
    )(d_act, before)
    d_low, d_high = edges(d_half)
    conv_parts = whole_call(kernel_grad_body, jax.ShapeDtypeStruct((10, conv_w), f32))(
        low, mixed_in, high, d_before
    )
    d_mixed = whole_call(d_mixed_body, jax.ShapeDtypeStruct(before.shape, bf16))(
        d_low, d_before, d_high, flat_kernel
    ).reshape(-1, conv_w)
    late = scatter_sum(dot_f32(flat_act, d_mixed, contract_rows))
    d_gate_frames = back[:, :inner_w]
    layer_out = back[:, inner_w : 2 * inner_w].reshape(activations.shape)
    d_raw_frames = back[:, 2 * inner_w :]
    grad_input = half(
        dot_f32(d_gate_frames, in_proj[:, :inner_w], contract_cols)
        + dot_f32(d_mixed, in_proj[:, inner_w:], contract_cols)
        + dot_f32(d_raw_frames, step_proj, contract_cols)
    ).reshape(activations.shape)
    grad_in_proj = jnp.concatenate([early[:, :inner_w], late], axis=1)
    grad_out_proj_t = early[:, inner_w : 2 * inner_w]
    grad_step_proj = early[:, 2 * inner_w :]
    small = jnp.concatenate(
        [conv_parts.reshape(-1), norm_part.reshape(-1), bias_part, rate_part, gain_part]
    )
    small = lax.psum(small, ("tm", "space"))
    taps = 9 * conv_w
    sizes = [taps, conv_w, inner_w, head_count, head_count, head_count]
    pieces, start = [], 0
    for size in sizes:
        pieces.append(small[start : start + size])
        start += size
    return (
        layer_out,
        grad_input,
        grad_in_proj,
        grad_step_proj,
        grad_out_proj_t,
        pieces[0].reshape(3, 3, conv_w),
        pieces[1],
        pieces[3],
        pieces[4],
        pieces[5],
        pieces[2],
    )


def solution(mesh):
    placed = (
        P("tm", "space", None, None),
        P(),
        P(),
        P(),
        P(),
        P(),
        P(),
        P(),
        P(),
        P(),
        P("tm", "space", None, None),
    )
    return jax.shard_map(
        on_device,
        mesh=mesh,
        in_specs=placed,
        out_specs=(
            P("tm", "space", None, None),
            P("tm", "space", None, None),
            P(("tm", "space"), None),
            P(("tm", "space"), None),
            P(("tm", "space"), None),
            P(),
            P(),
            P(),
            P(),
            P(),
            P(),
        ),
        check_vma=False,
    )
```

time: 672 us -> 330 us (0.49); the launches traced: 662 us -> 329 us
  matrix products: 197 us -> 26.3 us
  local copies, waits for them, and re-layouts: 139 us -> 34.8 us
  other arithmetic: 90.1 us -> 6.85 us
  waiting for transfers between devices: 140 us -> 161 us
    dot_general x57 -> x14, matrix products: 197 us -> 26.3 us  [the longest x12 24.4 us: dot_f32(): lax.dot_general(left, right, dims, preferred_element_type=jnp.float32)]
    dynamic_slice x32 -> x0, local copies, waits for them, and re-layouts: 42 us -> none  [ssd_sequence(): lax.scan(advance, start_state, (fold_blocks(heads_in), fold_blocks(b_proj...]
    dynamic_update_slice x28 -> x0, other arithmetic: 38.8 us -> none  [ssd_sequence(): lax.scan(advance, start_state, (fold_blocks(heads_in), fold_blocks(b_proj...]
    unnamed x2 -> x3, waiting for transfers between devices: 116 us -> 144 us
    reduce_sum x16 -> x0, local copies, waits for them, and re-layouts: 22.8 us -> none  [the longest x8 11.4 us: ssd_block(): spread = running[:, None] - running[None, :]]
    all_to_all x5 -> x3, waiting for transfers between devices: 19 us -> 0.01 us  [the longest x2 0.01 us: to_sequences(): got = lax.all_to_all(sent, 'tm', split_axis=0, concat_axis=0, tiled=True)]
    another operation x15 -> x0, other arithmetic: 15.7 us -> none  [the longest x8 13.2 us: ssd_block(): running = jnp.cumsum(decay_step, axis=0)]
    reduce_scatter x0 -> x1, waiting for transfers between devices: none -> 15.4 us  [scatter_sum(): lax.psum_scatter(half(partial), ('tm', 'space'), scatter_dimension=0, til...]
  transfers between devices with their start and end apart: 10 -> 9, of which waited for: 6 -> 4; matrix products, arithmetic and copies ran while one was open for 3% -> 14% of each run, Pallas kernels for 0% -> 0%
where the time goes in v1:
time: 330 us; the launch traced here: 329 us
  waiting for transfers between devices  161 us (49%)
  blocking collectives  57.9 us (18%)
  local copies, waits for them, and re-layouts  34.8 us (11%)
  matrix products  26.3 us (8%)
  starting transfers between devices  22.8 us (7%)
  between operations  14.6 us (4%)
  other arithmetic  6.85 us (2%)
  Pallas kernels  4.6 us (1%)
    unnamed x3, waiting for transfers between devices  144 us
    psum x1, blocking collectives, on_device(): small = lax.psum(small, ('tm', 'space'))  47.1 us
    dot_general x12, matrix products, dot_f32(): lax.dot_general(left, right, dims, preferred_element_type=jnp.float32)  24.4 us
    unnamed x70, local copies, waits for them, and re-layouts  20.2 us
    reduce_scatter x1, waiting for transfers between devices, scatter_sum(): lax.psum_scatter(half(partial), ('tm', 'space'), scatter_dimension=0, til...  15.4 us
    all_to_all x1, blocking collectives, to_frames(): lax.all_to_all(flat.reshape(parts, frames * few, width), 'tm', split_axis...  10.8 us
    all_to_all x2, starting transfers between devices, to_sequences(): got = lax.all_to_all(sent, 'tm', split_axis=0, concat_axis=0, tiled=True)  9.5 us
  transfers between devices with their start and end apart: 9, of which 4 were waited for; matrix products, arithmetic and copies ran while one was open for 14% of the time, Pallas kernels for 0%

profile of v1, /device:TPU:0, one launch (start us, length us, event | category | flops | bytes accessed | tf_op | source)
XLA Modules:
  0.0 328.5 jit_solution(16616111245265939060)
XLA Ops:
  7.2 1.2 pad_maximum_fusion.2
  9.0 1.1 copy.65
  10.2 5.3 %all-to-all-start.1 = ((bf16[4,32,2048]{2,1,0:T(8,128)(2,1)}), bf16[4,32,2048]{2,1,0:T(8,128)(2,1)}, u32[]{:S(2)}, u32[]{:S(2)}) async-start(bf16[4,32,2048]{2,1,0:T(8,128)(2,1)} %copy.65), calls=%async_computation.1 | async-start | bytes 1048576 | tf_op jit(solution)/shard_map/all_to_all | solution.py:230
  15.5 2.2 convolution_convert_fusion
  17.7 1.3 collective-permute-start.1
  19.0 3.0 collective-permute-start
  23.8 0.8 copy-done.9
  24.8 0.8 reshape.118
  25.6 4.2 %all-to-all-start = ((bf16[4,32,1152]{2,1,0:T(8,128)(2,1)}), bf16[4,32,1152]{2,1,0:T(8,128)(2,1)S(1)}, u32[]{:S(2)}, u32[]{:S(2)}) async-start(bf16[4,32,1152]{2,1,0:T(8,128)(2,1)} %reshape.118), calls=%async_computation | async-start | bytes 589824 | tf_op jit(solution)/shard_map/all_to_all | solution.py:230
  29.8 1.8 fusion.44
  32.0 1.8 fusion.17.d_normed_ref
  33.8 2.8 fusion.12.gate_ref
  36.7 0.9 copy-done.11
  38.3 2.1 shard_map.195
  40.5 10.8 %all_to_all.20 = bf16[4,32,1152]{2,1,0:T(8,128)(2,1)S(1)} all-to-all(bf16[4,32,1152]{2,1,0:T(8,128)(2,1)S(1)} %bitcast.84), channel_id=1, replica_groups=mesh['tm'=4,'space'=8] {'tm'}, dimensions={0} | all-to-all | bytes 589824 | tf_op jit(solution)/shard_map/all_to_all | solution.py:238
  51.7 1.1 copy-done.10
  53.0 1.3 collective-permute-start.3
  54.3 3.3 %collective-permute-start.2 = (bf16[8,1,8,1152]{3,2,1,0:T(8,128)(2,1)S(1)}, bf16[8,1,8,1152]{3,2,1,0:T(8,128)(2,1)S(1)}, u32[]{:S(2)}, u32[]{:S(2)}) collective-permute-start(bf16[8,1,8,1152]{3,2,1,0:T(8,128)(2,1)S(1)} %get-tuple-element.93), channel_id=1, source_target_pairs={{0,1},{1,2},{2,3},{3,4},{4,5},{5,6},{6,7},{8,9},{9,10},{10,11},{11... | collective-permute-start | bytes 442376 | tf_op jit(solution)/shard_map/ppermute | solution.py:219
  57.6 1.0 collective-permute-done.2.low_ref
  58.6 0.9 copy-done.4
  60.1 3.2 fusion
  63.3 4.3 %copy.79 = bf16[1024,1152]{1,0:T(8,128)(2,1)} copy(bf16[1024,1152]{0,1:T(8,128)(2,1)} %fusion) | data formatting | bytes 4718592
  67.7 1.5 copy.67
  69.2 1.7 fusion.48
  70.9 1.1 convolution_convert_fusion.4
  72.0 1.7 convolution_convert_fusion.2
  73.7 1.7 convolution_convert_fusion.1
  75.4 2.4 pad_maximum_fusion
  77.8 6.4 %copy.77 = bf16[1024,2064]{1,0:T(8,128)(2,1)} copy(bf16[1024,2064]{0,1:T(8,128)(2,1)} %pad_maximum_fusion) | data formatting | bytes 8454144
  85.0 1.4 convolution_convert_fusion.3
  86.4 0.8 pad_maximum_fusion.1
  87.2 4.3 %all-to-all-start.2 = ((bf16[4,32,2064]{2,1,0:T(8,128)(2,1)}), bf16[4,32,2064]{2,1,0:T(8,128)(2,1)}, u32[]{:S(2)}, u32[]{:S(2)}) async-start(bf16[4,32,2064]{2,1,0:T(8,128)(2,1)} %bitcast.88), calls=%async_computation.2 | async-start | bytes 1114112 | tf_op jit(solution)/shard_map/all_to_all | solution.py:238
  93.0 0.9 copy-done.6
  93.9 0.9 copy-done.8
  94.8 0.8 shard_map.198
  95.7 47.1 %psum.7 = f32[12592]{0:T(1024)S(1)} all-reduce(f32[12592]{0:T(1024)S(1)} %concatenate.20), channel_id=1, replica_groups=mesh['tm'=4,'space'=8] {'tm','space'}, use_global_device_ids=true, to_apply=%region_5.6 | all-reduce | flops 12592 | bytes 100736 | tf_op jit(solution)/shard_map/psum | solution.py:379
  145.3 1.3 copy.69
  146.9 1.1 reshape_reshape.18
  147.9 1.7 slice.86
  149.6 2.5 fusion.4
  152.2 2.6 fusion.8
  154.7 1.7 fusion.11
  156.4 15.4 %reduce-scatter.9.cloned.1.call-done = bf16[32,1152]{1,0:T(8,128)(2,1)} async-done(((bf16[1024,1152]{1,0:T(8,128)(2,1)}), bf16[32,1152]{1,0:T(8,128)(2,1)}) %reduce-scatter.9.cloned.1.call-update) | async-done | bytes 73744 | tf_op jit(solution)/shard_map/reduce_scatter | solution.py:246
  171.9 0.9 convert_element_type.61
  172.7 143.5 %reduce-scatter.7.cloned.1.call-done = bf16[32,2064]{1,0:T(8,128)(2,1)} async-done(((bf16[1024,2064]{1,0:T(8,128)(2,1)}), bf16[32,2064]{1,0:T(8,128)(2,1)}) %reduce-scatter.7.cloned.1.call-update) | async-done | bytes 132112
  316.2 1.2 copy.78
  318.0 0.9 fusion.49
  318.9 1.9 copy.75
  (105 shorter events, 11.3 us)
Async XLA Ops:
  7.2 24.8 %copy-start = (bf16[1024,1024]{1,0:T(8,128)(2,1)S(1)}, bf16[1024,1024]{1,0:T(8,128)(2,1)}, u32[]{:S(2)}) copy-start(bf16[1024,1024]{1,0:T(8,128)(2,1)} %param.20) | copy-start | bytes 6291460
  8.6 6.8 %copy-start.21 = (bf16[8,2,8,1024]{3,2,1,0:T(8,128)(2,1)S(1)}, bf16[8,2,8,1024]{3,2,1,0:T(8,128)(2,1)}, u32[]{:S(2)}) copy-start(bf16[8,2,8,1024]{3,2,1,0:T(8,128)(2,1)} %param.11) | copy-start | bytes 786436
  10.2 11.9 %copy-start.26 = (f32[1152]{0:T(1024)S(1)}, f32[1152]{0:T(1024)}, u32[]{:S(2)}) copy-start(f32[1152]{0:T(1024)} %param.17) | copy-start | bytes 13828
  10.2 11.9 %copy-start.28 = (f32[16]{0:T(128)S(1)}, f32[16]{0:T(128)}, u32[]{:S(2)}) copy-start(f32[16]{0:T(128)} %param.18) | copy-start | bytes 196
  10.2 12.1 %copy-start.23 = (f32[3,3,1152]{2,1,0:T(4,128)S(1)}, f32[3,3,1152]{2,1,0:T(4,128)}, u32[]{:S(2)}) copy-start(f32[3,3,1152]{2,1,0:T(4,128)} %param.16) | copy-start | bytes 124420
  10.2 15.4 %all-to-all-start.1 = ((bf16[4,32,2048]{2,1,0:T(8,128)(2,1)}), bf16[4,32,2048]{2,1,0:T(8,128)(2,1)}, u32[]{:S(2)}, u32[]{:S(2)}) async-start(bf16[4,32,2048]{2,1,0:T(8,128)(2,1)} %copy.65), calls=%async_computation.1 | async-start | bytes 1048576 | tf_op jit(solution)/shard_map/all_to_all | solution.py:230
  17.6 12.2 %copy-start.24 = (bf16[1024,16]{0,1:T(8,128)(2,1)S(1)}, bf16[1024,16]{0,1:T(8,128)(2,1)}, u32[]{:S(2)}) copy-start(bf16[1024,16]{0,1:T(8,128)(2,1)} %param.13) | copy-start | bytes 98308
  17.7 12.2 %copy-start.29 = (f32[16]{0:T(128)S(1)}, f32[16]{0:T(128)}, u32[]{:S(2)}) copy-start(f32[16]{0:T(128)} %param.14) | copy-start | bytes 196
  17.7 13.9 %copy-start.30 = (f32[16]{0:T(128)S(1)}, f32[16]{0:T(128)}, u32[]{:S(2)}) copy-start(f32[16]{0:T(128)} %param.15) | copy-start | bytes 196
  17.7 4.6 %collective-permute-start.1 = (bf16[8,1,8,1152]{3,2,1,0:T(8,128)(2,1)S(1)}, bf16[8,1,8,1152]{3,2,1,0:T(8,128)(2,1)S(1)}, u32[]{:S(2)}, u32[]{:S(2)}) collective-permute-start(bf16[8,1,8,1152]{3,2,1,0:T(8,128)(2,1)S(1)} %get-tuple-element.94), channel_id=1, source_target_pairs={{1,0},{2,1},{3,2},{4,3},{5,4},{6,5},{7,6},{9,8},{10,9},{11,10},{12... | collective-permute-start | bytes 442376 | tf_op jit(solution)/shard_map/ppermute | solution.py:220
  19.0 4.0 %collective-permute-start = (bf16[8,1,8,1152]{3,2,1,0:T(8,128)(2,1)S(1)}, bf16[8,1,8,1152]{3,2,1,0:T(8,128)(2,1)S(1)}, u32[]{:S(2)}, u32[]{:S(2)}) collective-permute-start(bf16[8,1,8,1152]{3,2,1,0:T(8,128)(2,1)S(1)} %get-tuple-element.95), channel_id=1, source_target_pairs={{0,1},{1,2},{2,3},{3,4},{4,5},{5,6},{6,7},{8,9},{9,10},{10,11},{11... | collective-permute-start | bytes 442376 | tf_op jit(solution)/shard_map/ppermute | solution.py:219
  22.3 3.3 %copy-start.3 = (f32[9,1152]{1,0:T(8,128)}, f32[9,1152]{1,0:T(8,128)S(1)}, u32[]{:S(2)}) copy-start(f32[9,1152]{1,0:T(8,128)S(1)} %reshape.116.kernel_ref) | copy-start | bytes 124420
  22.3 11.5 %copy-start.31 = (s32[128]{0:T(128)}, s32[128]{0:T(128)S(1)}, u32[]{:S(2)}) copy-start(s32[128]{0:T(128)S(1)} %and_select_fusion) | copy-start | bytes 1540
  22.3 3.3 %copy-start.5 = (bf16[8,1,8,1152]{3,2,1,0:T(8,128)(2,1)}, bf16[8,1,8,1152]{3,2,1,0:T(8,128)(2,1)S(1)}, u32[]{:S(2)}) copy-start(bf16[8,1,8,1152]{3,2,1,0:T(8,128)(2,1)S(1)} %collective-permute-done.1.high_ref) | copy-start | bytes 442372
  23.0 2.6 copy-start.7
  23.8 0.8 copy-start.9
  25.6 11.0 %all-to-all-start = ((bf16[4,32,1152]{2,1,0:T(8,128)(2,1)}), bf16[4,32,1152]{2,1,0:T(8,128)(2,1)S(1)}, u32[]{:S(2)}, u32[]{:S(2)}) async-start(bf16[4,32,1152]{2,1,0:T(8,128)(2,1)} %reshape.118), calls=%async_computation | async-start | bytes 589824 | tf_op jit(solution)/shard_map/all_to_all | solution.py:230
  29.8 142.0 %reduce-scatter.9.cloned.1.call-start = ((), (), s32[]{:S(2)}) async-start(), calls=%async_computation.7 | async-start | bytes 2433024 | tf_op jit(solution)/shard_map/reduce_scatter | solution.py:246
  31.6 5.0 %copy-start.32 = (f32[128,16]{0,1:T(8,128)}, f32[128,16]{0,1:T(8,128)S(1)}, u32[]{:S(2)}) copy-start(f32[128,16]{0,1:T(8,128)S(1)} %get-tuple-element.101) | copy-start | bytes 24580
  32.0 4.7 %copy-start.14 = (f32[1024]{0:T(1024)S(1)}, f32[1024]{0:T(1024)}, u32[]{:S(2)}) copy-start(f32[1024]{0:T(1024)} %param.19) | copy-start | bytes 12292
  36.6 1.0 copy-start.11
  37.6 0.7 copy-start.13
  40.4 11.0 %copy-start.1 = (bf16[128,1024]{1,0:T(8,128)(2,1)}, bf16[128,1024]{1,0:T(8,128)(2,1)S(1)}, u32[]{:S(2)}) copy-start(bf16[128,1024]{1,0:T(8,128)(2,1)S(1)} %get-tuple-element.24) | copy-start | bytes 786436
  40.4 11.0 %copy-start.12 = (f32[128,16]{1,0:T(8,128)}, f32[128,16]{1,0:T(8,128)S(1)}, u32[]{:S(2)}) copy-start(f32[128,16]{1,0:T(8,128)S(1)} %get-tuple-element.26) | copy-start | bytes 24580
  40.5 11.0 %copy-start.15 = (f32[1,1024]{1,0:T(1,128)}, f32[1,1024]{1,0:T(1,128)S(1)}, u32[]{:S(2)}) copy-start(f32[1,1024]{1,0:T(1,128)S(1)} %get-tuple-element.32) | copy-start | bytes 12292
  40.5 11.0 %copy-start.17 = (f32[1,1024]{1,0:T(1,128)}, f32[1,1024]{1,0:T(1,128)S(1)}, u32[]{:S(2)}) copy-start(f32[1,1024]{1,0:T(1,128)S(1)} %get-tuple-element.31) | copy-start | bytes 12292
  40.5 11.0 %copy-start.19 = (f32[16,128]{1,0:T(8,128)}, f32[16,128]{1,0:T(8,128)S(1)}, u32[]{:S(2)}) copy-start(f32[16,128]{1,0:T(8,128)S(1)} %get-tuple-element.25) | copy-start | bytes 24580
  51.7 1.1 copy-start.10
  53.0 4.6 %collective-permute-start.3 = (bf16[8,1,8,1152]{3,2,1,0:T(8,128)(2,1)S(1)}, bf16[8,1,8,1152]{3,2,1,0:T(8,128)(2,1)S(1)}, u32[]{:S(2)}, u32[]{:S(2)}) collective-permute-start(bf16[8,1,8,1152]{3,2,1,0:T(8,128)(2,1)S(1)} %get-tuple-element.92), channel_id=1, source_target_pairs={{1,0},{2,1},{3,2},{4,3},{5,4},{6,5},{7,6},{9,8},{10,9},{11,10},{12... | collective-permute-start | bytes 442376 | tf_op jit(solution)/shard_map/ppermute | solution.py:220
  54.3 4.3 %collective-permute-start.2 = (bf16[8,1,8,1152]{3,2,1,0:T(8,128)(2,1)S(1)}, bf16[8,1,8,1152]{3,2,1,0:T(8,128)(2,1)S(1)}, u32[]{:S(2)}, u32[]{:S(2)}) collective-permute-start(bf16[8,1,8,1152]{3,2,1,0:T(8,128)(2,1)S(1)} %get-tuple-element.93), channel_id=1, source_target_pairs={{0,1},{1,2},{2,3},{3,4},{4,5},{5,6},{6,7},{8,9},{9,10},{10,11},{11... | collective-permute-start | bytes 442376 | tf_op jit(solution)/shard_map/ppermute | solution.py:219
  58.6 0.9 copy-start.4
  67.6 1.6 copy-start.20
  67.7 248.6 %reduce-scatter.7.cloned.1.call-start = ((), (), s32[]{:S(2)}) async-start(), calls=%async_computation.6 | async-start | bytes 4595712
  69.2 4.5 %copy-start.2 = (bf16[128,1024]{1,0:T(8,128)(2,1)S(1)}, bf16[128,1024]{1,0:T(8,128)(2,1)}, u32[]{:S(2)}) copy-start(bf16[128,1024]{1,0:T(8,128)(2,1)} %copy-done.1) | copy-start | bytes 786436
  84.9 1.4 copy-start.22
  84.9 7.1 %copy-start.16 = (f32[1,1024]{1,0:T(1,128)S(1)}, f32[1,1024]{1,0:T(1,128)}, u32[]{:S(2)}) copy-start(f32[1,1024]{1,0:T(1,128)} %copy-done.15) | copy-start | bytes 12292
  86.4 9.3 %copy-start.18 = (f32[1,1024]{1,0:T(1,128)S(1)}, f32[1,1024]{1,0:T(1,128)}, u32[]{:S(2)}) copy-start(f32[1,1024]{1,0:T(1,128)} %copy-done.17) | copy-start | bytes 12292
  86.4 9.3 %copy-start.27 = (f32[16]{0:T(128)S(1)}, f32[16]{0:T(128)}, u32[]{:S(2)}) copy-start(f32[16]{0:T(128)} %get-tuple-element.99) | copy-start | bytes 196
  87.2 58.1 %all-to-all-start.2 = ((bf16[4,32,2064]{2,1,0:T(8,128)(2,1)}), bf16[4,32,2064]{2,1,0:T(8,128)(2,1)}, u32[]{:S(2)}, u32[]{:S(2)}) async-start(bf16[4,32,2064]{2,1,0:T(8,128)(2,1)} %bitcast.88), calls=%async_computation.2 | async-start | bytes 1114112 | tf_op jit(solution)/shard_map/all_to_all | solution.py:238
  93.0 0.9 copy-start.6
  93.9 0.9 copy-start.8
  152.2 2.6 copy-start.25
Sparse Core Ops, SparseCore 0:
  67.8 104.0 reduce-scatter.8
  174.2 141.9 reduce-scatter.6

commit v2 on v1

--- a/solution.py
+++ b/solution.py
@@ -242,10 +242,47 @@
     return got.reshape(frames, parts * few, width)
 
 
-def scatter_sum(partial):
-    return lax.psum_scatter(
-        half(partial), ("tm", "space"), scatter_dimension=0, tiled=True
-    ).astype(jnp.float32)
+def swapped_over(block, axis, bit):
+    pairs = [(i, i ^ (1 << bit)) for i in range(lax.axis_size(axis))]
+    return lax.ppermute(block, axis, pairs)
+
+
+def halve(block, dim, axis, bit):
+    mine = lax.rem(lax.axis_index(axis) // (1 << bit), 2)
+    sent = half(lax.dynamic_index_in_dim(block, 1 - mine, dim, keepdims=False))
+    kept = lax.dynamic_index_in_dim(block, mine, dim, keepdims=False)
+    return kept + swapped_over(sent, axis, bit).astype(jnp.float32)
+
+
+def bits_of(axis):
+    return lax.axis_size(axis).bit_length() - 1
+
+
+def scatter_sum(first, second):
+    tm_bits, space_bits = bits_of("tm"), bits_of("space")
+    devices = 1 << (tm_bits + space_bits)
+
+    def split(block):
+        block = block.reshape(
+            (2,) * (tm_bits + space_bits) + (block.shape[0] // devices, block.shape[1])
+        )
+        return halve(block, tm_bits + space_bits - 1, "space", 0)
+
+    first, second = split(first), split(second)
+    for step in range(tm_bits):
+        first = halve(first, tm_bits - 1 - step, "tm", step)
+        second = halve(second, 0, "tm", tm_bits - 1 - step)
+    joined = jnp.concatenate([first, second], axis=-1)
+    for bit in range(1, space_bits):
+        joined = halve(joined, space_bits - 1 - bit, "space", bit)
+    return joined
+
+
+def sum_everywhere(block):
+    for axis in ("space", "tm"):
+        for bit in range(bits_of(axis)):
+            block = block + swapped_over(block, axis, bit)
+    return block
 
 
 def on_device(
@@ -337,14 +374,8 @@
     back = to_frames(jnp.concatenate([d_gate, layer_seq, d_raw_half], axis=1), frame_count)
     back = back.reshape(-1, back.shape[-1])
     early = scatter_sum(
-        jnp.concatenate(
-            [
-                dot_f32(x_seq, d_gate, contract_rows),
-                dot_f32(cot_seq, normed, contract_rows),
-                dot_f32(x_seq, d_raw_half, contract_rows),
-            ],
-            axis=1,
-        )
+        dot_f32(x_seq, jnp.concatenate([d_gate, d_raw_half], axis=1), contract_rows),
+        dot_f32(cot_seq, normed, contract_rows),
     )
 
     d_before, d_half = whole_call(
@@ -361,7 +392,11 @@
     d_mixed = whole_call(d_mixed_body, jax.ShapeDtypeStruct(before.shape, bf16))(
         d_low, d_before, d_high, flat_kernel
     ).reshape(-1, conv_w)
-    late = scatter_sum(dot_f32(flat_act, d_mixed, contract_rows))
+    cut = conv_w // (2 * LANES) * LANES
+    late = scatter_sum(
+        dot_f32(flat_act, d_mixed[:, :cut], contract_rows),
+        dot_f32(flat_act, d_mixed[:, cut:], contract_rows),
+    )
     d_gate_frames = back[:, :inner_w]
     layer_out = back[:, inner_w : 2 * inner_w].reshape(activations.shape)
     d_raw_frames = back[:, 2 * inner_w :]
@@ -371,12 +406,12 @@
         + dot_f32(d_raw_frames, step_proj, contract_cols)
     ).reshape(activations.shape)
     grad_in_proj = jnp.concatenate([early[:, :inner_w], late], axis=1)
-    grad_out_proj_t = early[:, inner_w : 2 * inner_w]
-    grad_step_proj = early[:, 2 * inner_w :]
+    grad_step_proj = early[:, inner_w : inner_w + head_count]
+    grad_out_proj_t = early[:, inner_w + head_count :]
     small = jnp.concatenate(
         [conv_parts.reshape(-1), norm_part.reshape(-1), bias_part, rate_part, gain_part]
     )
-    small = lax.psum(small, ("tm", "space"))
+    small = sum_everywhere(small)
     taps = 9 * conv_w
     sizes = [taps, conv_w, inner_w, head_count, head_count, head_count]
     pieces, start = [], 0

time: 330 us -> 160 us (0.48)
  waiting for transfers between devices: 161 us -> 29.1 us
  blocking collectives: 57.9 us -> 0 us
  starting transfers between devices: 22.8 us -> 52 us
  between operations: 14.6 us -> 1.56 us
  other arithmetic: 6.85 us -> 12.4 us
    unnamed x3 -> x0, waiting for transfers between devices: 144 us -> none
    psum x1 -> x0, blocking collectives: 47.1 us -> none  [on_device(): small = lax.psum(small, ('tm', 'space'))]
    ppermute x0 -> x21, waiting for transfers between devices: none -> 29 us  [swapped_over(): return lax.ppermute(block, axis, pairs)]
    ppermute x0 -> x21, starting transfers between devices: none -> 25.2 us  [swapped_over(): return lax.ppermute(block, axis, pairs)]
    reduce_scatter x1 -> x0, waiting for transfers between devices: 15.4 us -> none  [scatter_sum(): lax.psum_scatter(half(partial), ('tm', 'space'), scatter_dimension=0, til...]
    unnamed x70 -> x77, local copies, waits for them, and re-layouts: 20.2 us -> 5.54 us
    all_to_all x1 -> x0, blocking collectives: 10.8 us -> none  [to_frames(): lax.all_to_all(flat.reshape(parts, frames * few, width), 'tm', split_axis...]
    convert_element_type x1 -> x15, local copies, waits for them, and re-layouts: 0.72 us -> 10.5 us  [half(): return value.astype(jnp.bfloat16)]
  transfers between devices with their start and end apart: 9 -> 29, of which waited for: 4 -> 8; matrix products, arithmetic and copies ran while one was open for 14% -> 33% of each run, Pallas kernels for 0% -> 2%
where the time goes in v2:
time: 160 us; the launch traced here: 159 us
  starting transfers between devices  52 us (32%)
  local copies, waits for them, and re-layouts  34 us (21%)
  waiting for transfers between devices  29.1 us (18%)
  matrix products  25 us (16%)
  other arithmetic  12.4 us (8%)
  Pallas kernels  4.6 us (3%)
    ppermute x21, waiting for transfers between devices, swapped_over(): return lax.ppermute(block, axis, pairs)  29 us
    ppermute x21, starting transfers between devices, swapped_over(): return lax.ppermute(block, axis, pairs)  25.2 us
    dot_general x12, matrix products, dot_f32(): lax.dot_general(left, right, dims, preferred_element_type=jnp.float32)  23.7 us
    convert_element_type x15, local copies, waits for them, and re-layouts, half(): return value.astype(jnp.bfloat16)  10.5 us
    all_to_all x2, starting transfers between devices, to_sequences(): got = lax.all_to_all(sent, 'tm', split_axis=0, concat_axis=0, tiled=True)  9.36 us
    all_to_all x2, starting transfers between devices, to_frames(): lax.all_to_all(flat.reshape(parts, frames * few, width), 'tm', split_axis...  8.5 us
    add x16, other arithmetic, halve(): return kept + swapped_over(sent, axis, bit).astype(jnp.float32)  7.14 us
    ppermute x2, starting transfers between devices, edges(): low = lax.ppermute(block[:, -1:], 'space', forward)  6.26 us
  transfers between devices with their start and end apart: 29, of which 8 were waited for; matrix products, arithmetic and copies ran while one was open for 33% of the time, Pallas kernels for 2%

profile of v2, /device:TPU:0, one launch (start us, length us, event | category | flops | bytes accessed | tf_op | source)
XLA Modules:
  0.0 158.7 jit_solution(5498682402242920631)
XLA Ops:
  0.7 2.0 %pad_maximum_fusion.1 = bf16[8,2,8,2048]{3,2,1,0:T(8,128)(2,1)} fusion(bf16[8,2,8,1024]{3,2,1,0:T(8,128)(2,1)} %param.21, bf16[8,2,8,1024]{3,2,1,0:T(8,128)(2,1)} %param.11), kind=kLoop, calls=%fused_computation.52 | loop fusion | flops 1048576 | bytes 1048576 | tf_op jit(solution)/shard_map/concatenate | solution.py:313
  5.5 5.2 %all-to-all-start.1 = ((bf16[4,32,2048]{2,1,0:T(8,128)(2,1)}), bf16[4,32,2048]{2,1,0:T(8,128)(2,1)}, u32[]{:S(2)}, u32[]{:S(2)}) async-start(bf16[4,32,2048]{2,1,0:T(8,128)(2,1)} %copy.68), calls=%async_computation.1 | async-start | bytes 1048576 | tf_op jit(solution)/shard_map/all_to_all | solution.py:230
  10.7 2.2 %convolution_convert_fusion = bf16[128,1152]{1,0:T(8,128)(2,1)S(1)} fusion(bf16[128,1024]{1,0:T(8,128)(2,1)S(1)} %bitcast.168, bf16[1024,2176]{1,0:T(8,128)(2,1)} %param.12), kind=kOutput, calls=%fused_computation | convolution fusion | flops 302137344 | bytes 2916352 | tf_op jit(solution)/shard_map/dot_general | solution.py:20
  14.3 3.0 %collective-permute-start = (bf16[8,1,8,1152]{3,2,1,0:T(8,128)(2,1)S(1)}, bf16[8,1,8,1152]{3,2,1,0:T(8,128)(2,1)S(1)}, u32[]{:S(2)}, u32[]{:S(2)}) collective-permute-start(bf16[8,1,8,1152]{3,2,1,0:T(8,128)(2,1)S(1)} %get-tuple-element.82), channel_id=1, source_target_pairs={{0,1},{1,2},{2,3},{3,4},{4,5},{5,6},{6,7},{8,9},{9,10},{10,11},{11... | collective-permute-start | bytes 442376 | tf_op jit(solution)/shard_map/ppermute | solution.py:219
  20.9 4.2 %all-to-all-start = ((bf16[4,32,1152]{2,1,0:T(8,128)(2,1)}), bf16[4,32,1152]{2,1,0:T(8,128)(2,1)S(1)}, u32[]{:S(2)}, u32[]{:S(2)}) async-start(bf16[4,32,1152]{2,1,0:T(8,128)(2,1)} %reshape.146), calls=%async_computation | async-start | bytes 589824 | tf_op jit(solution)/shard_map/all_to_all | solution.py:230
  25.1 1.8 %fusion.75 = (f32[16,128]{1,0:T(8,128)}, f32[128,16]{0,1:T(8,128)S(1)}) fusion(f32[16]{0:T(128)S(1)} %copy-done.29, bf16[1024,16]{0,1:T(8,128)(2,1)S(1)} %copy-done.25, bf16[128,2048]{1,0:T(8,128)(2,1)} %bitcast.6), kind=kOutput, calls=%fused_computation.123 | convolution fusion | flops 4212736 | bytes 311360 | tf_op jit(solution)/shard_map/dot_general | solution.py:20
  27.8 1.8 %fusion.42.d_normed_ref = f32[128,1024]{1,0:T(8,128)S(1)} fusion(bf16[1024,1024]{1,0:T(8,128)(2,1)S(1)} %copy-done, bf16[128,2048]{1,0:T(8,128)(2,1)} %bitcast.6), kind=kOutput, calls=%fused_computation.81 | convolution fusion | flops 268435456 | bytes 2883584 | tf_op jit(solution)/shard_map/dot_general | solution.py:20
  29.6 2.8 %fusion.11.gate_ref = bf16[128,1024]{1,0:T(8,128)(2,1)} fusion(bf16[1024,2176]{1,0:T(8,128)(2,1)} %param.12, bf16[128,2048]{1,0:T(8,128)(2,1)} %bitcast.6), kind=kOutput, calls=%fused_computation.23 | convolution fusion | flops 268566528 | bytes 2621440 | tf_op jit(solution)/shard_map/dot_general | solution.py:20
  36.3 2.1 %shard_map.195 = (bf16[128,1024]{1,0:T(8,128)(2,1)S(1)}, bf16[128,1024]{1,0:T(8,128)(2,1)S(1)}, bf16[128,1152]{1,0:T(8,128)(2,1)S(1)}, f32[128,16]{1,0:T(8,128)S...) custom-call(bf16[128,1152]{1,0:T(8,128)(2,1)S(1)} %bitcast.153, ...), custom_call_target="tpu_custom_call" | custom-call | tf_op jit(solution)/shard_map/pallas_call | solution.py:337
  39.0 3.7 %fusion.40 = f32[1024,1024]{1,0:T(8,128)} fusion(bf16[128,1024]{1,0:T(8,128)(2,1)S(1)} %get-tuple-element.24, bf16[128,2048]{1,0:T(8,128)(2,1)} %bitcast.6), kind=kOutput, calls=%fused_computation.79 | convolution fusion | flops 268435456 | bytes 4718592 | tf_op jit(solution)/shard_map/dot_general | solution.py:20
  43.3 1.3 reduce.3
  45.6 4.2 %all-to-all-start.3 = ((bf16[4,32,1152]{2,1,0:T(8,128)(2,1)}), bf16[4,32,1152]{2,1,0:T(8,128)(2,1)S(1)}, u32[]{:S(2)}, u32[]{:S(2)}) async-start(bf16[4,32,1152]{2,1,0:T(8,128)(2,1)} %bitcast.154), calls=%async_computation.3 | async-start | bytes 589824 | tf_op jit(solution)/shard_map/all_to_all | solution.py:238
  51.1 2.7 %fusion.15 = bf16[2,2,2,2,32,1024]{5,4,3,2,1,0:T(8,128)(2,1)} fusion(f32[2,2,2,2,2,32,1024]{6,5,4,3,2,1,0:T(8,128)} %bitcast.162, s32[]{:T(128)S(6)} %select_n.125), kind=kLoop, calls=%fused_computation.29 | loop fusion | bytes 2097156 | tf_op jit(solution)/shard_map/convert_element_type | solution.py:24
  53.8 1.8 %collective-permute-start.7 = (bf16[2,2,2,2,32,1024]{5,4,3,2,1,0:T(8,128)(2,1)}, bf16[2,2,2,2,32,1024]{5,4,3,2,1,0:T(8,128)(2,1)}, u32[]{:S(2)}, u32[]{:S(2)}) collective-permute-start(bf16[2,2,2,2,32,1024]{5,4,3,2,1,0:T(8,128)(2,1)} %fusion.15), channel_id=1, source_target_pairs={{0,1},{1,0},{2,3},{3,2},{4,5},{5,4},{6,7},{7,6},{8,9},{9,8},{10,11... | collective-permute-start | bytes 3145736 | tf_op jit(solution)/shard_map/ppermute | solution.py:247
  56.6 3.9 %fusion.32 = f32[1024,1040]{1,0:T(8,128)} fusion(bf16[128,16]{1,0:T(8,128)(2,1)S(1)} %copy.71, bf16[128,1024]{1,0:T(8,128)(2,1)S(1)} %get-tuple-element.23, bf16[128,2048]{1,0:T(8,128)(2,1)} %bitcast.6), kind=kOutput, calls=%fused_computation.66 | convolution fusion | flops 273162240 | bytes 4788224 | tf_op jit(solution)/shard_map/dot_general | solution.py:20
  60.5 4.3 %all-to-all-start.2 = ((bf16[4,32,2064]{2,1,0:T(8,128)(2,1)}), bf16[4,32,2064]{2,1,0:T(8,128)(2,1)}, u32[]{:S(2)}, u32[]{:S(2)}) async-start(bf16[4,32,2064]{2,1,0:T(8,128)(2,1)} %bitcast.11), calls=%async_computation.2 | async-start | bytes 1114112 | tf_op jit(solution)/shard_map/all_to_all | solution.py:238
  66.4 1.4 collective-permute-start.3
  67.8 3.2 %collective-permute-start.2 = (bf16[8,1,8,1152]{3,2,1,0:T(8,128)(2,1)S(1)}, bf16[8,1,8,1152]{3,2,1,0:T(8,128)(2,1)S(1)}, u32[]{:S(2)}, u32[]{:S(2)}) collective-permute-start(bf16[8,1,8,1152]{3,2,1,0:T(8,128)(2,1)S(1)} %get-tuple-element.80), channel_id=1, source_target_pairs={{0,1},{1,2},{2,3},{3,4},{4,5},{5,6},{6,7},{8,9},{9,10},{10,11},{11... | collective-permute-start | bytes 442376 | tf_op jit(solution)/shard_map/ppermute | solution.py:219
  71.1 3.7 %collective-permute-start.21 = (f32[12592]{0:T(1024)S(1)}, f32[12592]{0:T(1024)S(1)}, u32[]{:S(2)}, u32[]{:S(2)}) collective-permute-start(f32[12592]{0:T(1024)S(1)} %add.230), channel_id=1, source_target_pairs={{0,2},{1,3},{2,0},{3,1},{4,6},{5,7},{6,4},{7,5},{8,10},{9,11},{10,... | collective-permute-start | bytes 151112 | tf_op jit(solution)/shard_map/ppermute | solution.py:247
  74.8 2.8 %fusion.14 = bf16[2,2,2,2,32,1040]{5,4,3,2,1,0:T(8,128)(2,1)} fusion(f32[2,2,2,2,2,32,1040]{6,5,4,3,2,1,0:T(8,128)} %bitcast.158, s32[]{:T(128)S(6)} %select_n.125), kind=kLoop, calls=%fused_computation.25 | loop fusion | bytes 2129924 | tf_op jit(solution)/shard_map/convert_element_type | solution.py:24
  78.6 1.7 %collective-permute-start.22 = (f32[12592]{0:T(1024)S(1)}, f32[12592]{0:T(1024)S(1)}, u32[]{:S(2)}, u32[]{:S(2)}) collective-permute-start(f32[12592]{0:T(1024)S(1)} %add.231), channel_id=1, source_target_pairs={{0,4},{1,5},{2,6},{3,7},{4,0},{5,1},{6,2},{7,3},{8,12},{9,13},{10,... | collective-permute-start | bytes 151112 | tf_op jit(solution)/shard_map/ppermute | solution.py:247
  81.5 1.8 %copy.79 = f32[1024,512]{1,0:T(8,128)} copy(f32[1024,512]{0,1:T(8,128)S(1)} %convolution_bitcast_fusion.1) | data formatting | bytes 4194304 | tf_op jit(solution)/shard_map/dot_general | solution.py:20
  83.3 2.1 %fusion.24 = bf16[2,2,2,2,32,512]{5,4,3,2,1,0:T(8,128)(2,1)} fusion(f32[2,2,2,2,2,32,512]{6,5,4,3,2,1,0:T(8,128)} %bitcast.166, s32[]{:T(128)S(6)} %select_n.125), kind=kLoop, calls=%fused_computation.51 | loop fusion | bytes 1048580 | tf_op jit(solution)/shard_map/convert_element_type | solution.py:24
  86.2 2.1 %copy.80 = f32[1024,640]{1,0:T(8,128)} copy(f32[1024,640]{0,1:T(8,128)S(1)} %convolution_bitcast_fusion) | data formatting | bytes 5242880 | tf_op jit(solution)/shard_map/dot_general | solution.py:20
  88.3 2.2 %fusion.16 = bf16[2,2,2,2,32,640]{5,4,3,2,1,0:T(8,128)(2,1)} fusion(f32[2,2,2,2,2,32,640]{6,5,4,3,2,1,0:T(8,128)} %bitcast.164, s32[]{:T(128)S(6)} %select_n.125), kind=kLoop, calls=%fused_computation.38 | loop fusion | bytes 1310724 | tf_op jit(solution)/shard_map/convert_element_type | solution.py:24
  90.8 2.1 %collective-permute-start.23 = (f32[12592]{0:T(1024)S(1)}, f32[12592]{0:T(1024)S(1)}, u32[]{:S(2)}, u32[]{:S(2)}) collective-permute-start(f32[12592]{0:T(1024)S(1)} %add.232), channel_id=1, source_target_pairs={{0,8},{8,0},{16,24},{24,16},{1,9},{9,1},{17,25},{25,17},{2,10},{10... | collective-permute-start | bytes 151112 | tf_op jit(solution)/shard_map/ppermute | solution.py:247
  92.9 1.3 copy.72
  94.7 2.6 %fusion.3 = f32[128,1024]{1,0:T(8,128)S(1)} fusion(bf16[1024,2176]{1,0:T(8,128)(2,1)} %param.12, bf16[128,2064]{1,0:T(8,128)(2,1)S(1)} %reshape_reshape.18), kind=kOutput, calls=%fused_computation.8 | convolution fusion | flops 268435456 | bytes 2883584 | tf_op jit(solution)/shard_map/dot_general | solution.py:20
  97.4 2.6 %fusion.7 = f32[128,1024]{1,0:T(8,128)S(1)} fusion(f32[128,1024]{1,0:T(8,128)S(1)} %fusion.3, bf16[128,1152]{1,0:T(8,128)(2,1)S(1)} %bitcast.149, bf16[1024,2176]{1,0:T(8,128)(2,1)} %param.12), kind=kOutput, calls=%fused_computation.21 | convolution fusion | flops 302120960 | bytes 3702784 | tf_op jit(solution)/shard_map/dot_general | solution.py:20
  100.0 1.5 collective-permute-start.24
  102.4 1.8 %slice.94 = bf16[128,1024]{1,0:T(8,128)(2,1)} slice(bf16[128,2064]{1,0:T(8,128)(2,1)} %copy-done.23), slice={[0:128], [1024:2048]} | slice | bytes 524288 | tf_op jit(solution)/shard_map/slice | solution.py:401
  106.7 1.5 bitcast_add_fusion.4
  109.0 1.6 bitcast_add_fusion.2
  110.6 1.5 collective-permute-start.16
  112.1 1.7 %bitcast_add_fusion.1 = f32[2,2,2,2,32,1024]{5,4,3,2,1,0:T(8,128)S(1)} fusion(bf16[2,2,2,2,32,1024]{5,4,3,2,1,0:T(8,128)(2,1)} %collective-permute-done.7, f32[2,2,2,2,2,32,1024]{6,5,4,3,2,1,0:T(8,128)S(1)} %bitcast.163, s32[]{:T(128)S(6)} %select_n.124), kind=kLoop, calls=%fused_computation.4 | loop fusion | flops 1048576 | bytes 5242884 | tf_op jit(solution)/shard_map/add | solution.py:254
  114.6 1.5 bitcast_add_fusion
  116.2 1.3 collective-permute-start.5
  117.6 1.5 collective-permute-start.14
  119.1 2.2 %collective-permute-done.16 = bf16[2,2,2,32,640]{4,3,2,1,0:T(8,128)(2,1)S(1)} collective-permute-done((bf16[2,2,2,32,640]{4,3,2,1,0:T(8,128)(2,1)S(1)}, bf16[2,2,2,32,640]{4,3,2,1,0:T(8,128)(2,1)S(1)}, u32[]{:S(2)}, u32[]{:S(2)}) %collective-permute-start.16) | collective-permute-done | bytes 327712 | tf_op jit(solution)/shard_map/ppermute | solution.py:247
  121.4 1.3 collective-permute-start.17
  122.8 10.8 %collective-permute-done.14 = bf16[2,2,32,512]{3,2,1,0:T(8,128)(2,1)S(1)} collective-permute-done((bf16[2,2,32,512]{3,2,1,0:T(8,128)(2,1)S(1)}, bf16[2,2,32,512]{3,2,1,0:T(8,128)(2,1)S(1)}, u32[]{:S(2)}, u32[]{:S(2)}) %collective-permute-start.14) | collective-permute-done | bytes 131104 | tf_op jit(solution)/shard_map/ppermute | solution.py:247
  133.9 1.5 collective-permute-start.9
  136.2 1.8 %collective-permute-start.18 = (bf16[2,32,1152]{2,1,0:T(8,128)(2,1)S(1)}, bf16[2,32,1152]{2,1,0:T(8,128)(2,1)S(1)}, u32[]{:S(2)}, u32[]{:S(2)}) collective-permute-start(bf16[2,32,1152]{2,1,0:T(8,128)(2,1)S(1)} %fusion.49), channel_id=1, source_target_pairs={{0,2},{1,3},{2,0},{3,1},{4,6},{5,7},{6,4},{7,5},{8,10},{9,11},{10,... | collective-permute-start | bytes 442376 | tf_op jit(solution)/shard_map/ppermute | solution.py:247
  138.0 2.5 %collective-permute-done.9 = bf16[2,2,32,1024]{3,2,1,0:T(8,128)(2,1)S(1)} collective-permute-done((bf16[2,2,32,1024]{3,2,1,0:T(8,128)(2,1)S(1)}, bf16[2,2,32,1024]{3,2,1,0:T(8,128)(2,1)S(1)}, u32[]{:S(2)}, u32[]{:S(2)}) %collective-permute-start.9) | collective-permute-done | bytes 262176 | tf_op jit(solution)/shard_map/ppermute | solution.py:247
  140.5 2.1 %collective-permute-done.6 = bf16[2,2,32,1040]{3,2,1,0:T(8,128)(2,1)S(1)} collective-permute-done((bf16[2,2,32,1040]{3,2,1,0:T(8,128)(2,1)S(1)}, bf16[2,2,32,1040]{3,2,1,0:T(8,128)(2,1)S(1)}, u32[]{:S(2)}, u32[]{:S(2)}) %collective-permute-start.6) | collective-permute-done | bytes 266272 | tf_op jit(solution)/shard_map/ppermute | solution.py:247
  142.8 1.5 collective-permute-start.10
  144.9 5.4 %collective-permute-done.10 = bf16[2,32,2064]{2,1,0:T(8,128)(2,1)S(1)} collective-permute-done((bf16[2,32,2064]{2,1,0:T(8,128)(2,1)S(1)}, bf16[2,32,2064]{2,1,0:T(8,128)(2,1)S(1)}, u32[]{:S(2)}, u32[]{:S(2)}) %collective-permute-start.10) | collective-permute-done | bytes 264224 | tf_op jit(solution)/shard_map/ppermute | solution.py:247
  150.7 5.7 %collective-permute-done.11 = bf16[32,2064]{1,0:T(8,128)(2,1)S(1)} collective-permute-done((bf16[32,2064]{1,0:T(8,128)(2,1)S(1)}, bf16[32,2064]{1,0:T(8,128)(2,1)S(1)}, u32[]{:S(2)}, u32[]{:S(2)}) %collective-permute-start.11) | collective-permute-done | bytes 132128 | tf_op jit(solution)/shard_map/ppermute | solution.py:247
  (185 shorter events, 31.3 us)
Async XLA Ops:
  0.6 27.2 %copy-start = (bf16[1024,1024]{1,0:T(8,128)(2,1)S(1)}, bf16[1024,1024]{1,0:T(8,128)(2,1)}, u32[]{:S(2)}) copy-start(bf16[1024,1024]{1,0:T(8,128)(2,1)} %param.20) | copy-start | bytes 6291460
  2.7 8.0 %copy-start.21 = (bf16[8,2,8,1024]{3,2,1,0:T(8,128)(2,1)S(1)}, bf16[8,2,8,1024]{3,2,1,0:T(8,128)(2,1)}, u32[]{:S(2)}) copy-start(bf16[8,2,8,1024]{3,2,1,0:T(8,128)(2,1)} %param.11) | copy-start | bytes 786436
  5.5 15.4 %all-to-all-start.1 = ((bf16[4,32,2048]{2,1,0:T(8,128)(2,1)}), bf16[4,32,2048]{2,1,0:T(8,128)(2,1)}, u32[]{:S(2)}, u32[]{:S(2)}) async-start(bf16[4,32,2048]{2,1,0:T(8,128)(2,1)} %copy.68), calls=%async_computation.1 | async-start | bytes 1048576 | tf_op jit(solution)/shard_map/all_to_all | solution.py:230
  10.7 6.7 %copy-start.27 = (f32[1152]{0:T(1024)S(1)}, f32[1152]{0:T(1024)}, u32[]{:S(2)}) copy-start(f32[1152]{0:T(1024)} %param.17) | copy-start | bytes 13828
  10.7 6.8 %copy-start.28 = (f32[16]{0:T(128)S(1)}, f32[16]{0:T(128)}, u32[]{:S(2)}) copy-start(f32[16]{0:T(128)} %param.18) | copy-start | bytes 196
  10.7 7.5 %copy-start.24 = (f32[3,3,1152]{2,1,0:T(4,128)S(1)}, f32[3,3,1152]{2,1,0:T(4,128)}, u32[]{:S(2)}) copy-start(f32[3,3,1152]{2,1,0:T(4,128)} %param.16) | copy-start | bytes 124420
  12.9 12.2 %copy-start.25 = (bf16[1024,16]{0,1:T(8,128)(2,1)S(1)}, bf16[1024,16]{0,1:T(8,128)(2,1)}, u32[]{:S(2)}) copy-start(bf16[1024,16]{0,1:T(8,128)(2,1)} %param.13) | copy-start | bytes 98308
  12.9 12.2 %copy-start.29 = (f32[16]{0:T(128)S(1)}, f32[16]{0:T(128)}, u32[]{:S(2)}) copy-start(f32[16]{0:T(128)} %param.14) | copy-start | bytes 196
  12.9 13.9 %copy-start.30 = (f32[16]{0:T(128)S(1)}, f32[16]{0:T(128)}, u32[]{:S(2)}) copy-start(f32[16]{0:T(128)} %param.15) | copy-start | bytes 196
  13.0 5.3 %collective-permute-start.1 = (bf16[8,1,8,1152]{3,2,1,0:T(8,128)(2,1)S(1)}, bf16[8,1,8,1152]{3,2,1,0:T(8,128)(2,1)S(1)}, u32[]{:S(2)}, u32[]{:S(2)}) collective-permute-start(bf16[8,1,8,1152]{3,2,1,0:T(8,128)(2,1)S(1)} %get-tuple-element.81), channel_id=1, source_target_pairs={{1,0},{2,1},{3,2},{4,3},{5,4},{6,5},{7,6},{9,8},{10,9},{11,10},{12... | collective-permute-start | bytes 442376 | tf_op jit(solution)/shard_map/ppermute | solution.py:220
  14.3 4.0 %collective-permute-start = (bf16[8,1,8,1152]{3,2,1,0:T(8,128)(2,1)S(1)}, bf16[8,1,8,1152]{3,2,1,0:T(8,128)(2,1)S(1)}, u32[]{:S(2)}, u32[]{:S(2)}) collective-permute-start(bf16[8,1,8,1152]{3,2,1,0:T(8,128)(2,1)S(1)} %get-tuple-element.82), channel_id=1, source_target_pairs={{0,1},{1,2},{2,3},{3,4},{4,5},{5,6},{6,7},{8,9},{9,10},{10,11},{11... | collective-permute-start | bytes 442376 | tf_op jit(solution)/shard_map/ppermute | solution.py:219
  18.2 11.4 %copy-start.32 = (s32[128]{0:T(128)}, s32[128]{0:T(128)S(1)}, u32[]{:S(2)}) copy-start(s32[128]{0:T(128)S(1)} %and_select_fusion) | copy-start | bytes 1540
  18.3 8.8 %copy-start.2 = (bf16[8,1,8,1152]{3,2,1,0:T(8,128)(2,1)}, bf16[8,1,8,1152]{3,2,1,0:T(8,128)(2,1)S(1)}, u32[]{:S(2)}) copy-start(bf16[8,1,8,1152]{3,2,1,0:T(8,128)(2,1)S(1)} %collective-permute-done.1.high_ref) | copy-start | bytes 442372
  18.3 8.8 %copy-start.4 = (bf16[8,1,8,1152]{3,2,1,0:T(8,128)(2,1)}, bf16[8,1,8,1152]{3,2,1,0:T(8,128)(2,1)S(1)}, u32[]{:S(2)}) copy-start(bf16[8,1,8,1152]{3,2,1,0:T(8,128)(2,1)S(1)} %collective-permute-done.low_ref) | copy-start | bytes 442372
  20.9 11.6 %all-to-all-start = ((bf16[4,32,1152]{2,1,0:T(8,128)(2,1)}), bf16[4,32,1152]{2,1,0:T(8,128)(2,1)S(1)}, u32[]{:S(2)}, u32[]{:S(2)}) async-start(bf16[4,32,1152]{2,1,0:T(8,128)(2,1)} %reshape.146), calls=%async_computation | async-start | bytes 589824 | tf_op jit(solution)/shard_map/all_to_all | solution.py:230
  39.0 10.8 %copy-start.31 = (f32[16]{0:T(128)S(1)}, f32[16]{0:T(128)}, u32[]{:S(2)}) copy-start(f32[16]{0:T(128)} %param.15) | copy-start | bytes 196
  39.0 10.8 %copy-start.33 = (s32[128]{0:T(128)S(1)}, s32[128]{0:T(128)}, u32[]{:S(2)}) copy-start(s32[128]{0:T(128)} %copy-done.32) | copy-start | bytes 1540
  39.0 10.8 %copy-start.35 = (f32[128,16]{0,1:T(8,128)S(1)}, f32[128,16]{0,1:T(8,128)}, u32[]{:S(2)}) copy-start(f32[128,16]{0,1:T(8,128)} %copy-done.34) | copy-start | bytes 24580
  45.6 14.9 %all-to-all-start.3 = ((bf16[4,32,1152]{2,1,0:T(8,128)(2,1)}), bf16[4,32,1152]{2,1,0:T(8,128)(2,1)S(1)}, u32[]{:S(2)}, u32[]{:S(2)}) async-start(bf16[4,32,1152]{2,1,0:T(8,128)(2,1)} %bitcast.154), calls=%async_computation.3 | async-start | bytes 589824 | tf_op jit(solution)/shard_map/all_to_all | solution.py:238
  53.8 58.3 %collective-permute-start.7 = (bf16[2,2,2,2,32,1024]{5,4,3,2,1,0:T(8,128)(2,1)}, bf16[2,2,2,2,32,1024]{5,4,3,2,1,0:T(8,128)(2,1)}, u32[]{:S(2)}, u32[]{:S(2)}) collective-permute-start(bf16[2,2,2,2,32,1024]{5,4,3,2,1,0:T(8,128)(2,1)} %fusion.15), channel_id=1, source_target_pairs={{0,1},{1,0},{2,3},{3,2},{4,5},{5,4},{6,7},{7,6},{8,9},{9,8},{10,11... | collective-permute-start | bytes 3145736 | tf_op jit(solution)/shard_map/ppermute | solution.py:247
  60.5 32.4 %all-to-all-start.2 = ((bf16[4,32,2064]{2,1,0:T(8,128)(2,1)}), bf16[4,32,2064]{2,1,0:T(8,128)(2,1)}, u32[]{:S(2)}, u32[]{:S(2)}) async-start(bf16[4,32,2064]{2,1,0:T(8,128)(2,1)} %bitcast.11), calls=%async_computation.2 | async-start | bytes 1114112 | tf_op jit(solution)/shard_map/all_to_all | solution.py:238
  66.3 4.7 %collective-permute-start.20 = (f32[12592]{0:T(1024)S(1)}, f32[12592]{0:T(1024)S(1)}, u32[]{:S(2)}, u32[]{:S(2)}) collective-permute-start(f32[12592]{0:T(1024)S(1)} %concatenate.27), channel_id=1, source_target_pairs={{0,1},{1,0},{2,3},{3,2},{4,5},{5,4},{6,7},{7,6},{8,9},{9,8},{10,11... | collective-permute-start | bytes 151112 | tf_op jit(solution)/shard_map/ppermute | solution.py:247
  66.4 14.6 %copy-start.22 = (bf16[8,2,8,1024]{3,2,1,0:T(8,128)(2,1)S(1)}, bf16[8,2,8,1024]{3,2,1,0:T(8,128)(2,1)}, u32[]{:S(2)}) copy-start(bf16[8,2,8,1024]{3,2,1,0:T(8,128)(2,1)} %param.11) | copy-start | bytes 786436
  66.4 13.9 %collective-permute-start.3 = (bf16[8,1,8,1152]{3,2,1,0:T(8,128)(2,1)S(1)}, bf16[8,1,8,1152]{3,2,1,0:T(8,128)(2,1)S(1)}, u32[]{:S(2)}, u32[]{:S(2)}) collective-permute-start(bf16[8,1,8,1152]{3,2,1,0:T(8,128)(2,1)S(1)} %get-tuple-element.79), channel_id=1, source_target_pairs={{1,0},{2,1},{3,2},{4,3},{5,4},{6,5},{7,6},{9,8},{10,9},{11,10},{12... | collective-permute-start | bytes 442376 | tf_op jit(solution)/shard_map/ppermute | solution.py:220
  67.8 12.5 %collective-permute-start.2 = (bf16[8,1,8,1152]{3,2,1,0:T(8,128)(2,1)S(1)}, bf16[8,1,8,1152]{3,2,1,0:T(8,128)(2,1)S(1)}, u32[]{:S(2)}, u32[]{:S(2)}) collective-permute-start(bf16[8,1,8,1152]{3,2,1,0:T(8,128)(2,1)S(1)} %get-tuple-element.80), channel_id=1, source_target_pairs={{0,1},{1,2},{2,3},{3,4},{4,5},{5,6},{6,7},{8,9},{9,10},{10,11},{11... | collective-permute-start | bytes 442376 | tf_op jit(solution)/shard_map/ppermute | solution.py:219
  71.1 7.6 %collective-permute-start.21 = (f32[12592]{0:T(1024)S(1)}, f32[12592]{0:T(1024)S(1)}, u32[]{:S(2)}, u32[]{:S(2)}) collective-permute-start(f32[12592]{0:T(1024)S(1)} %add.230), channel_id=1, source_target_pairs={{0,2},{1,3},{2,0},{3,1},{4,6},{5,7},{6,4},{7,5},{8,10},{9,11},{10,... | collective-permute-start | bytes 151112 | tf_op jit(solution)/shard_map/ppermute | solution.py:247
  77.6 36.9 %collective-permute-start.4 = (bf16[2,2,2,2,32,1040]{5,4,3,2,1,0:T(8,128)(2,1)}, bf16[2,2,2,2,32,1040]{5,4,3,2,1,0:T(8,128)(2,1)}, u32[]{:S(2)}, u32[]{:S(2)}) collective-permute-start(bf16[2,2,2,2,32,1040]{5,4,3,2,1,0:T(8,128)(2,1)} %fusion.14), channel_id=1, source_target_pairs={{0,1},{1,0},{2,3},{3,2},{4,5},{5,4},{6,7},{7,6},{8,9},{9,8},{10,11... | collective-permute-start | bytes 3194888 | tf_op jit(solution)/shard_map/ppermute | solution.py:247
  78.6 12.2 %collective-permute-start.22 = (f32[12592]{0:T(1024)S(1)}, f32[12592]{0:T(1024)S(1)}, u32[]{:S(2)}, u32[]{:S(2)}) collective-permute-start(f32[12592]{0:T(1024)S(1)} %add.231), channel_id=1, source_target_pairs={{0,4},{1,5},{2,6},{3,7},{4,0},{5,1},{6,2},{7,3},{8,12},{9,13},{10,... | collective-permute-start | bytes 151112 | tf_op jit(solution)/shard_map/ppermute | solution.py:247
  85.4 21.3 %collective-permute-start.12 = (bf16[2,2,2,2,32,512]{5,4,3,2,1,0:T(8,128)(2,1)}, bf16[2,2,2,2,32,512]{5,4,3,2,1,0:T(8,128)(2,1)}, u32[]{:S(2)}, u32[]{:S(2)}) collective-permute-start(bf16[2,2,2,2,32,512]{5,4,3,2,1,0:T(8,128)(2,1)} %fusion.24), channel_id=1, source_target_pairs={{0,1},{1,0},{2,3},{3,2},{4,5},{5,4},{6,7},{7,6},{8,9},{9,8},{10,11... | collective-permute-start | bytes 1572872 | tf_op jit(solution)/shard_map/ppermute | solution.py:247
  90.5 18.4 %collective-permute-start.15 = (bf16[2,2,2,2,32,640]{5,4,3,2,1,0:T(8,128)(2,1)}, bf16[2,2,2,2,32,640]{5,4,3,2,1,0:T(8,128)(2,1)}, u32[]{:S(2)}, u32[]{:S(2)}) collective-permute-start(bf16[2,2,2,2,32,640]{5,4,3,2,1,0:T(8,128)(2,1)} %fusion.16), channel_id=1, source_target_pairs={{0,1},{1,0},{2,3},{3,2},{4,5},{5,4},{6,7},{7,6},{8,9},{9,8},{10,11... | collective-permute-start | bytes 1966088 | tf_op jit(solution)/shard_map/ppermute | solution.py:247
  90.8 9.1 %collective-permute-start.23 = (f32[12592]{0:T(1024)S(1)}, f32[12592]{0:T(1024)S(1)}, u32[]{:S(2)}, u32[]{:S(2)}) collective-permute-start(f32[12592]{0:T(1024)S(1)} %add.232), channel_id=1, source_target_pairs={{0,8},{8,0},{16,24},{24,16},{1,9},{9,1},{17,25},{25,17},{2,10},{10... | collective-permute-start | bytes 151112 | tf_op jit(solution)/shard_map/ppermute | solution.py:247
  94.7 6.8 %copy-start.23 = (bf16[128,2064]{1,0:T(8,128)(2,1)}, bf16[128,2064]{1,0:T(8,128)(2,1)S(1)}, u32[]{:S(2)}) copy-start(bf16[128,2064]{1,0:T(8,128)(2,1)S(1)} %reshape_reshape.18) | copy-start | bytes 1585156
  100.0 4.3 %collective-permute-start.24 = (f32[12592]{0:T(1024)S(1)}, f32[12592]{0:T(1024)S(1)}, u32[]{:S(2)}, u32[]{:S(2)}) collective-permute-start(f32[12592]{0:T(1024)S(1)} %add.233), channel_id=1, source_target_pairs={{0,16},{8,24},{16,0},{24,8},{1,17},{9,25},{17,1},{25,9},{2,18},{10... | collective-permute-start | bytes 151112 | tf_op jit(solution)/shard_map/ppermute | solution.py:247
  102.4 6.5 %copy-start.20 = (f32[1024,640]{1,0:T(8,128)S(1)}, f32[1024,640]{1,0:T(8,128)}, u32[]{:S(2)}) copy-start(f32[1024,640]{1,0:T(8,128)} %copy.80) | copy-start | bytes 7864324
  102.4 12.1 %slice-start = ((s8[4718592]{0:T(1024)(128)(4,1)}), s8[524288]{0:T(1024)(128)(4,1)S(1)}, s32[]{:S(2)}) async-start(s8[4718592]{0:T(1024)(128)(4,1)} %bitcast.159), calls=%async_computation.4 | async-start | bytes 1048576
  108.3 9.2 %collective-permute-start.13 = (bf16[2,2,2,32,512]{4,3,2,1,0:T(8,128)(2,1)S(1)}, bf16[2,2,2,32,512]{4,3,2,1,0:T(8,128)(2,1)S(1)}, u32[]{:S(2)}, u32[]{:S(2)}) collective-permute-start(bf16[2,2,2,32,512]{4,3,2,1,0:T(8,128)(2,1)S(1)} %fusion.38), channel_id=1, source_target_pairs={{0,8},{8,0},{16,24},{24,16},{1,9},{9,1},{17,25},{25,17},{2,10},{10... | collective-permute-start | bytes 786440 | tf_op jit(solution)/shard_map/ppermute | solution.py:247
  110.6 10.7 %collective-permute-start.16 = (bf16[2,2,2,32,640]{4,3,2,1,0:T(8,128)(2,1)S(1)}, bf16[2,2,2,32,640]{4,3,2,1,0:T(8,128)(2,1)S(1)}, u32[]{:S(2)}, u32[]{:S(2)}) collective-permute-start(bf16[2,2,2,32,640]{4,3,2,1,0:T(8,128)(2,1)S(1)} %fusion.25), channel_id=1, source_target_pairs={{0,16},{8,24},{16,0},{24,8},{1,17},{9,25},{17,1},{25,9},{2,18},{10... | collective-permute-start | bytes 983048 | tf_op jit(solution)/shard_map/ppermute | solution.py:247
  113.9 19.9 %collective-permute-start.8 = (bf16[2,2,2,32,1024]{4,3,2,1,0:T(8,128)(2,1)S(1)}, bf16[2,2,2,32,1024]{4,3,2,1,0:T(8,128)(2,1)S(1)}, u32[]{:S(2)}, u32[]{:S(2)}) collective-permute-start(bf16[2,2,2,32,1024]{4,3,2,1,0:T(8,128)(2,1)S(1)} %fusion.23), channel_id=1, source_target_pairs={{0,16},{8,24},{16,0},{24,8},{1,17},{9,25},{17,1},{25,9},{2,18},{10... | collective-permute-start | bytes 1572872 | tf_op jit(solution)/shard_map/ppermute | solution.py:247
  116.2 19.2 %collective-permute-start.5 = (bf16[2,2,2,32,1040]{4,3,2,1,0:T(8,128)(2,1)S(1)}, bf16[2,2,2,32,1040]{4,3,2,1,0:T(8,128)(2,1)S(1)}, u32[]{:S(2)}, u32[]{:S(2)}) collective-permute-start(bf16[2,2,2,32,1040]{4,3,2,1,0:T(8,128)(2,1)S(1)} %fusion.17), channel_id=1, source_target_pairs={{0,8},{8,0},{16,24},{24,16},{1,9},{9,1},{17,25},{25,17},{2,10},{10... | collective-permute-start | bytes 1597448 | tf_op jit(solution)/shard_map/ppermute | solution.py:247
  117.6 15.9 %collective-permute-start.14 = (bf16[2,2,32,512]{3,2,1,0:T(8,128)(2,1)S(1)}, bf16[2,2,32,512]{3,2,1,0:T(8,128)(2,1)S(1)}, u32[]{:S(2)}, u32[]{:S(2)}) collective-permute-start(bf16[2,2,32,512]{3,2,1,0:T(8,128)(2,1)S(1)} %fusion.51), channel_id=1, source_target_pairs={{0,16},{8,24},{16,0},{24,8},{1,17},{9,25},{17,1},{25,9},{2,18},{10... | collective-permute-start | bytes 393224 | tf_op jit(solution)/shard_map/ppermute | solution.py:247
  121.4 12.2 %collective-permute-start.17 = (bf16[2,2,32,640]{3,2,1,0:T(8,128)(2,1)S(1)}, bf16[2,2,32,640]{3,2,1,0:T(8,128)(2,1)S(1)}, u32[]{:S(2)}, u32[]{:S(2)}) collective-permute-start(bf16[2,2,32,640]{3,2,1,0:T(8,128)(2,1)S(1)} %fusion.47), channel_id=1, source_target_pairs={{0,8},{8,0},{16,24},{24,16},{1,9},{9,1},{17,25},{25,17},{2,10},{10... | collective-permute-start | bytes 491528 | tf_op jit(solution)/shard_map/ppermute | solution.py:247
  133.9 6.6 %collective-permute-start.9 = (bf16[2,2,32,1024]{3,2,1,0:T(8,128)(2,1)S(1)}, bf16[2,2,32,1024]{3,2,1,0:T(8,128)(2,1)S(1)}, u32[]{:S(2)}, u32[]{:S(2)}) collective-permute-start(bf16[2,2,32,1024]{3,2,1,0:T(8,128)(2,1)S(1)} %fusion.37), channel_id=1, source_target_pairs={{0,8},{8,0},{16,24},{24,16},{1,9},{9,1},{17,25},{25,17},{2,10},{10... | collective-permute-start | bytes 786440 | tf_op jit(solution)/shard_map/ppermute | solution.py:247
  135.6 7.1 %collective-permute-start.6 = (bf16[2,2,32,1040]{3,2,1,0:T(8,128)(2,1)S(1)}, bf16[2,2,32,1040]{3,2,1,0:T(8,128)(2,1)S(1)}, u32[]{:S(2)}, u32[]{:S(2)}) collective-permute-start(bf16[2,2,32,1040]{3,2,1,0:T(8,128)(2,1)S(1)} %fusion.26), channel_id=1, source_target_pairs={{0,16},{8,24},{16,0},{24,8},{1,17},{9,25},{17,1},{25,9},{2,18},{10... | collective-permute-start | bytes 798728 | tf_op jit(solution)/shard_map/ppermute | solution.py:247
  136.2 8.2 %collective-permute-start.18 = (bf16[2,32,1152]{2,1,0:T(8,128)(2,1)S(1)}, bf16[2,32,1152]{2,1,0:T(8,128)(2,1)S(1)}, u32[]{:S(2)}, u32[]{:S(2)}) collective-permute-start(bf16[2,32,1152]{2,1,0:T(8,128)(2,1)S(1)} %fusion.49), channel_id=1, source_target_pairs={{0,2},{1,3},{2,0},{3,1},{4,6},{5,7},{6,4},{7,5},{8,10},{9,11},{10,... | collective-permute-start | bytes 442376 | tf_op jit(solution)/shard_map/ppermute | solution.py:247
  142.8 7.4 %collective-permute-start.10 = (bf16[2,32,2064]{2,1,0:T(8,128)(2,1)S(1)}, bf16[2,32,2064]{2,1,0:T(8,128)(2,1)S(1)}, u32[]{:S(2)}, u32[]{:S(2)}) collective-permute-start(bf16[2,32,2064]{2,1,0:T(8,128)(2,1)S(1)} %fusion.36), channel_id=1, source_target_pairs={{0,2},{1,3},{2,0},{3,1},{4,6},{5,7},{6,4},{7,5},{8,10},{9,11},{10,... | collective-permute-start | bytes 792584 | tf_op jit(solution)/shard_map/ppermute | solution.py:247
  144.4 14.3 %copy-start.1 = (bf16[1024,1024]{1,0:T(8,128)(2,1)S(1)}, bf16[1024,1024]{1,0:T(8,128)(2,1)}, u32[]{:S(2)}) copy-start(bf16[1024,1024]{1,0:T(8,128)(2,1)} %param.20) | copy-start | bytes 6291460
  144.5 6.3 %collective-permute-start.19 = (bf16[32,1152]{1,0:T(8,128)(2,1)S(1)}, bf16[32,1152]{1,0:T(8,128)(2,1)S(1)}, u32[]{:S(2)}, u32[]{:S(2)}) collective-permute-start(bf16[32,1152]{1,0:T(8,128)(2,1)S(1)} %fusion.53), channel_id=1, source_target_pairs={{0,4},{1,5},{2,6},{3,7},{4,0},{5,1},{6,2},{7,3},{8,12},{9,13},{10,... | collective-permute-start | bytes 221192 | tf_op jit(solution)/shard_map/ppermute | solution.py:247
  150.5 6.0 %collective-permute-start.11 = (bf16[32,2064]{1,0:T(8,128)(2,1)S(1)}, bf16[32,2064]{1,0:T(8,128)(2,1)S(1)}, u32[]{:S(2)}, u32[]{:S(2)}) collective-permute-start(bf16[32,2064]{1,0:T(8,128)(2,1)S(1)} %fusion.50), channel_id=1, source_target_pairs={{0,4},{1,5},{2,6},{3,7},{4,0},{5,1},{6,2},{7,3},{8,12},{9,13},{10,... | collective-permute-start | bytes 396296 | tf_op jit(solution)/shard_map/ppermute | solution.py:247
  (19 other events, 61.7 us)

commit v3 on v2

--- a/solution.py
+++ b/solution.py
@@ -258,21 +258,20 @@
     return lax.axis_size(axis).bit_length() - 1
 
 
-def scatter_sum(first, second):
-    tm_bits, space_bits = bits_of("tm"), bits_of("space")
-    devices = 1 << (tm_bits + space_bits)
-
-    def split(block):
-        block = block.reshape(
-            (2,) * (tm_bits + space_bits) + (block.shape[0] // devices, block.shape[1])
-        )
-        return halve(block, tm_bits + space_bits - 1, "space", 0)
-
-    first, second = split(first), split(second)
-    for step in range(tm_bits):
-        first = halve(first, tm_bits - 1 - step, "tm", step)
-        second = halve(second, 0, "tm", tm_bits - 1 - step)
-    joined = jnp.concatenate([first, second], axis=-1)
+def core_halves(block):
+    bits = bits_of("tm") + bits_of("space")
+    block = block.reshape((2,) * bits + (block.shape[0] >> bits, block.shape[1]))
+    return halve(block, bits - 1, "space", 0)
+
+
+def tm_step(pair, step):
+    last = bits_of("tm") - 1
+    return [halve(pair[0], last - step, "tm", step), halve(pair[1], 0, "tm", last - step)]
+
+
+def chip_rows(pair):
+    joined = jnp.concatenate(pair, axis=-1)
+    space_bits = bits_of("space")
     for bit in range(1, space_bits):
         joined = halve(joined, space_bits - 1 - bit, "space", bit)
     return joined
@@ -361,7 +360,6 @@
         norm_gain.reshape(1, -1),
     )
     d_act = to_frames(d_act_seq, frame_count).reshape(grid + (conv_w,))
-    layer_seq = half(dot_f32(normed, out_proj))
     col_turned = col_sums.T
     d_running = col_turned * steps - row_sums
     d_decay = jnp.dot(earlier.T, d_running, precision=top_precision)
@@ -371,12 +369,12 @@
     d_raw = d_steps * jax.nn.sigmoid(step_raw)
     bias_part = jnp.sum(d_raw, axis=0)
     d_raw_half = half(d_raw)
-    back = to_frames(jnp.concatenate([d_gate, layer_seq, d_raw_half], axis=1), frame_count)
-    back = back.reshape(-1, back.shape[-1])
-    early = scatter_sum(
-        dot_f32(x_seq, jnp.concatenate([d_gate, d_raw_half], axis=1), contract_rows),
-        dot_f32(cot_seq, normed, contract_rows),
-    )
+    early = [
+        core_halves(dot_f32(x_seq, jnp.concatenate([d_gate, d_raw_half], axis=1), contract_rows)),
+        core_halves(dot_f32(cot_seq, normed, contract_rows)),
+    ]
+    d_act, early = lax.optimization_barrier((d_act, early))
+    early = tm_step(early, 0)
 
     d_before, d_half = whole_call(
         d_before_body,
@@ -393,10 +391,27 @@
         d_low, d_before, d_high, flat_kernel
     ).reshape(-1, conv_w)
     cut = conv_w // (2 * LANES) * LANES
-    late = scatter_sum(
-        dot_f32(flat_act, d_mixed[:, :cut], contract_rows),
-        dot_f32(flat_act, d_mixed[:, cut:], contract_rows),
-    )
+    d_mixed, early = lax.optimization_barrier((d_mixed, early))
+    late = core_halves(dot_f32(flat_act, d_mixed, contract_rows))
+    for step in range(1, bits_of("tm")):
+        early = tm_step(early, step)
+    small = jnp.concatenate(
+        [conv_parts.reshape(-1), norm_part.reshape(-1), bias_part, rate_part, gain_part]
+    )
+
+    late, early, normed, d_gate, d_raw_half, d_mixed = lax.optimization_barrier(
+        (late, early, normed, d_gate, d_raw_half, d_mixed)
+    )
+    early = chip_rows(early)
+    late = [late[..., :cut], late[..., cut:]]
+    for step in range(bits_of("tm")):
+        late = tm_step(late, step)
+        if step == 0:
+            late, small = lax.optimization_barrier((late, small))
+    late = chip_rows(late)
+    layer_seq = half(dot_f32(normed, out_proj))
+    back = to_frames(jnp.concatenate([d_gate, layer_seq, d_raw_half], axis=1), frame_count)
+    back = back.reshape(-1, back.shape[-1])
     d_gate_frames = back[:, :inner_w]
     layer_out = back[:, inner_w : 2 * inner_w].reshape(activations.shape)
     d_raw_frames = back[:, 2 * inner_w :]
@@ -408,9 +423,6 @@
     grad_in_proj = jnp.concatenate([early[:, :inner_w], late], axis=1)
     grad_step_proj = early[:, inner_w : inner_w + head_count]
     grad_out_proj_t = early[:, inner_w + head_count :]
-    small = jnp.concatenate(
-        [conv_parts.reshape(-1), norm_part.reshape(-1), bias_part, rate_part, gain_part]
-    )
     small = sum_everywhere(small)
     taps = 9 * conv_w
     sizes = [taps, conv_w, inner_w, head_count, head_count, head_count]

time: 160 us -> 181 us (1.13)
  local copies, waits for them, and re-layouts: 34 us -> 47.1 us
  other arithmetic: 12.4 us -> 23.2 us
  waiting for transfers between devices: 29.1 us -> 25.8 us
    unnamed x77 -> x113, local copies, waits for them, and re-layouts: 5.54 us -> 16.7 us
    ppermute x21 -> x20, waiting for transfers between devices: 29 us -> 18.5 us  [swapped_over(): return lax.ppermute(block, axis, pairs)]
    add x16 -> x15, other arithmetic: 7.14 us -> 16.4 us  [halve(): return kept + swapped_over(sent, axis, bit).astype(jnp.float32)]
    all_to_all x2, waiting for transfers between devices: 0.01 us -> 6.21 us  [to_frames(): lax.all_to_all(flat.reshape(parts, frames * few, width), 'tm', split_axis...]
    dot_general x2 -> x0, local copies, waits for them, and re-layouts: 3.93 us -> none  [dot_f32(): lax.dot_general(left, right, dims, preferred_element_type=jnp.float32)]
    convert_element_type x15 -> x14, local copies, waits for them, and re-layouts: 10.5 us -> 13.7 us  [half(): return value.astype(jnp.bfloat16)]
    slice x0 -> x2, local copies, waits for them, and re-layouts: none -> 2.3 us  [on_device(): late = [late[..., :cut], late[..., cut:]]]
    ppermute x21 -> x20, starting transfers between devices: 25.2 us -> 24.5 us  [swapped_over(): return lax.ppermute(block, axis, pairs)]
  transfers between devices with their start and end apart: 29 -> 28, of which waited for: 8 -> 9; matrix products, arithmetic and copies ran while one was open for 33% -> 29% of each run, Pallas kernels for 2% -> 1%
where the time goes in v3:
time: 181 us; the launch traced here: 179 us
  starting transfers between devices  50.8 us (28%)
  local copies, waits for them, and re-layouts  47.1 us (26%)
  waiting for transfers between devices  25.8 us (14%)
  matrix products  25.4 us (14%)
  other arithmetic  23.2 us (13%)
  Pallas kernels  5.3 us (3%)
    ppermute x20, starting transfers between devices, swapped_over(): return lax.ppermute(block, axis, pairs)  24.5 us
    dot_general x11, matrix products, dot_f32(): lax.dot_general(left, right, dims, preferred_element_type=jnp.float32)  23.6 us
    ppermute x20, waiting for transfers between devices, swapped_over(): return lax.ppermute(block, axis, pairs)  18.5 us
    unnamed x113, local copies, waits for them, and re-layouts  16.7 us
    add x15, other arithmetic, halve(): return kept + swapped_over(sent, axis, bit).astype(jnp.float32)  16.4 us
    convert_element_type x14, local copies, waits for them, and re-layouts, half(): return value.astype(jnp.bfloat16)  13.7 us
    all_to_all x2, starting transfers between devices, to_sequences(): got = lax.all_to_all(sent, 'tm', split_axis=0, concat_axis=0, tiled=True)  9.37 us
    all_to_all x2, starting transfers between devices, to_frames(): lax.all_to_all(flat.reshape(parts, frames * few, width), 'tm', split_axis...  8.05 us
  transfers between devices with their start and end apart: 28, of which 9 were waited for; matrix products, arithmetic and copies ran while one was open for 29% of the time, Pallas kernels for 1%

profile of v3, /device:TPU:0, one launch (start us, length us, event | category | flops | bytes accessed | tf_op | source)
XLA Modules:
  0.0 179.1 jit_solution(1447233703663617211)
XLA Ops:
  3.6 5.2 %all-to-all-start.1 = ((bf16[4,32,2048]{2,1,0:T(8,128)(2,1)}), bf16[4,32,2048]{2,1,0:T(8,128)(2,1)}, u32[]{:S(2)}, u32[]{:S(2)}) async-start(bf16[4,32,2048]{2,1,0:T(8,128)(2,1)} %copy.66), calls=%async_computation.1 | async-start | bytes 1048576 | tf_op jit(solution)/shard_map/all_to_all | solution.py:230
  8.8 2.2 %convolution_convert_fusion = bf16[128,1152]{1,0:T(8,128)(2,1)S(1)} fusion(bf16[128,1024]{1,0:T(8,128)(2,1)S(1)} %bitcast.156, bf16[1024,2176]{1,0:T(8,128)(2,1)} %param.12), kind=kOutput, calls=%fused_computation | convolution fusion | flops 302137344 | bytes 2916352 | tf_op jit(solution)/shard_map/dot_general | solution.py:20
  11.1 1.3 collective-permute-start.1
  12.4 3.0 %collective-permute-start = (bf16[8,1,8,1152]{3,2,1,0:T(8,128)(2,1)S(1)}, bf16[8,1,8,1152]{3,2,1,0:T(8,128)(2,1)S(1)}, u32[]{:S(2)}, u32[]{:S(2)}) collective-permute-start(bf16[8,1,8,1152]{3,2,1,0:T(8,128)(2,1)S(1)} %get-tuple-element.114), channel_id=1, source_target_pairs={{0,1},{1,2},{2,3},{3,4},{4,5},{5,6},{6,7},{8,9},{9,10},{10,11},{11... | collective-permute-start | bytes 442376 | tf_op jit(solution)/shard_map/ppermute | solution.py:219
  19.0 4.2 %all-to-all-start = ((bf16[4,32,1152]{2,1,0:T(8,128)(2,1)}), bf16[4,32,1152]{2,1,0:T(8,128)(2,1)S(1)}, u32[]{:S(2)}, u32[]{:S(2)}) async-start(bf16[4,32,1152]{2,1,0:T(8,128)(2,1)} %reshape.142), calls=%async_computation | async-start | bytes 589824 | tf_op jit(solution)/shard_map/all_to_all | solution.py:230
  23.2 1.8 fusion.72
  25.3 1.8 fusion.41.d_normed_ref
  27.2 2.8 %fusion.11.gate_ref = bf16[128,1024]{1,0:T(8,128)(2,1)} fusion(bf16[1024,2176]{1,0:T(8,128)(2,1)} %param.12, bf16[128,2048]{1,0:T(8,128)(2,1)} %bitcast.6), kind=kOutput, calls=%fused_computation.21 | convolution fusion | flops 268566528 | bytes 2621440 | tf_op jit(solution)/shard_map/dot_general | solution.py:20
  31.7 2.8 %shard_map.195 = (bf16[128,1024]{1,0:T(8,128)(2,1)S(1)}, bf16[128,1024]{1,0:T(8,128)(2,1)S(1)}, bf16[128,1152]{1,0:T(8,128)(2,1)}, f32[128,16]{1,0:T(8,128)S(1)}...) custom-call(bf16[128,1152]{1,0:T(8,128)(2,1)S(1)} %bitcast.145, ...), custom_call_target="tpu_custom_call" | custom-call | tf_op jit(solution)/shard_map/pallas_call | solution.py:336
  38.5 1.7 fusion.77
  40.3 3.8 %fusion.39 = f32[1024,1024]{1,0:T(8,128)} fusion(bf16[128,1024]{1,0:T(8,128)(2,1)} %copy-done.1, bf16[128,2048]{1,0:T(8,128)(2,1)} %bitcast.6), kind=kOutput, calls=%fused_computation.74 | convolution fusion | flops 268435456 | bytes 4718592 | tf_op jit(solution)/shard_map/dot_general | solution.py:20
  44.1 2.7 %fusion.16 = bf16[2,2,2,2,32,1024]{5,4,3,2,1,0:T(8,128)(2,1)} fusion(f32[2,2,2,2,2,32,1024]{6,5,4,3,2,1,0:T(8,128)} %bitcast.17, s32[]{:T(128)S(6)} %select_n.121), kind=kLoop, calls=%fused_computation.28 | loop fusion | bytes 2097156 | tf_op jit(solution)/shard_map/convert_element_type | solution.py:24
  46.8 2.4 %collective-permute-start.3 = (bf16[2,2,2,2,32,1024]{5,4,3,2,1,0:T(8,128)(2,1)}, bf16[2,2,2,2,32,1024]{5,4,3,2,1,0:T(8,128)(2,1)}, u32[]{:S(2)}, u32[]{:S(2)}) collective-permute-start(bf16[2,2,2,2,32,1024]{5,4,3,2,1,0:T(8,128)(2,1)} %fusion.16), channel_id=1, source_target_pairs={{0,1},{1,0},{2,3},{3,2},{4,5},{5,4},{6,7},{7,6},{8,9},{9,8},{10,11... | collective-permute-start | bytes 3145736 | tf_op jit(solution)/shard_map/ppermute | solution.py:247
  49.2 1.7 fusion.31
  51.0 2.2 %copy-done.25 = f32[1024,1040]{1,0:T(8,128)} copy-done((f32[1024,1040]{1,0:T(8,128)}, f32[1024,1040]{1,0:T(8,128)S(1)}, u32[]{:S(2)}) %copy-start.25) | copy-done | bytes 4259864
  54.4 3.9 %all-to-all-start.2 = ((bf16[4,32,1152]{2,1,0:T(8,128)(2,1)}), bf16[4,32,1152]{2,1,0:T(8,128)(2,1)S(1)}, u32[]{:S(2)}, u32[]{:S(2)}) async-start(bf16[4,32,1152]{2,1,0:T(8,128)(2,1)} %bitcast.10), calls=%async_computation.2 | async-start | bytes 589824 | tf_op jit(solution)/shard_map/all_to_all | solution.py:238
  58.3 6.2 %all-to-all-done.2 = bf16[4,32,1152]{2,1,0:T(8,128)(2,1)S(1)} async-done(((bf16[4,32,1152]{2,1,0:T(8,128)(2,1)}), bf16[4,32,1152]{2,1,0:T(8,128)(2,1)S(1)}, u32[]{:S(2)}, u32[]{:S(2)}) %all-to-all-start.2) | async-done | bytes 294944 | tf_op jit(solution)/shard_map/all_to_all | solution.py:238
  64.9 2.4 %bitcast_add_fusion.2 = f32[2,2,2,2,32,1024]{5,4,3,2,1,0:T(8,128)S(1)} fusion(bf16[2,2,2,2,32,1024]{5,4,3,2,1,0:T(8,128)(2,1)} %collective-permute-done.3, f32[2,2,2,2,2,32,1024]{6,5,4,3,2,1,0:T(8,128)} %bitcast.17, s32[]{:T(128)S(6)} %select_n.120), kind=kLoop, calls=%fused_computation.6 | loop fusion | flops 1048576 | bytes 5242884 | tf_op jit(solution)/shard_map/add | solution.py:254
  68.1 1.5 bitcast_add_fusion.1
  70.6 1.4 collective-permute-start.7
  74.5 1.3 collective-permute-start.5
  75.8 3.2 %collective-permute-start.4 = (bf16[8,1,8,1152]{3,2,1,0:T(8,128)(2,1)}, bf16[8,1,8,1152]{3,2,1,0:T(8,128)(2,1)S(1)}, u32[]{:S(2)}, u32[]{:S(2)}) collective-permute-start(bf16[8,1,8,1152]{3,2,1,0:T(8,128)(2,1)} %get-tuple-element.112), channel_id=1, source_target_pairs={{0,1},{1,2},{2,3},{3,4},{4,5},{5,6},{6,7},{8,9},{9,10},{10,11},{11... | collective-permute-start | bytes 442376 | tf_op jit(solution)/shard_map/ppermute | solution.py:219
  84.1 1.5 bitcast_add_fusion.4
  85.6 2.0 %collective-permute-done.6 = bf16[2,2,2,32,1040]{4,3,2,1,0:T(8,128)(2,1)} collective-permute-done((bf16[2,2,2,32,1040]{4,3,2,1,0:T(8,128)(2,1)}, bf16[2,2,2,32,1040]{4,3,2,1,0:T(8,128)(2,1)}, u32[]{:S(2)}, u32[]{:S(2)}) %collective-permute-start.6) | collective-permute-done | bytes 532512 | tf_op jit(solution)/shard_map/ppermute | solution.py:247
  88.9 3.0 %fusion.82 = f32[1152,1024]{0,1:T(8,128)} fusion(bf16[128,1152]{1,0:T(8,128)(2,1)S(1)} %bitcast.140, bf16[128,1024]{1,0:T(8,128)(2,1)S(1)} %bitcast.157), kind=kOutput, calls=%fused_computation.127 | convolution fusion | flops 301989888 | bytes 5275648 | tf_op jit(solution)/shard_map/dot_general | solution.py:20
  91.9 2.9 %fusion.15 = bf16[2,2,2,2,32,1152]{5,4,2,3,1,0:T(8,128)(2,1)} fusion(f32[2,2,2,2,2,32,1152]{6,5,4,3,2,1,0:T(8,128)} %bitcast.26, s32[]{:T(128)S(6)} %select_n.121), kind=kLoop, calls=%fused_computation.24 | loop fusion | bytes 2359300 | tf_op jit(solution)/shard_map/convert_element_type | solution.py:24
  94.8 2.2 %collective-permute-start.8 = (bf16[2,2,2,2,32,1152]{5,4,2,3,1,0:T(8,128)(2,1)}, bf16[2,2,2,2,32,1152]{5,4,2,3,1,0:T(8,128)(2,1)}, u32[]{:S(2)}, u32[]{:S(2)}) collective-permute-start(bf16[2,2,2,2,32,1152]{5,4,2,3,1,0:T(8,128)(2,1)} %fusion.15), channel_id=1, source_target_pairs={{0,1},{1,0},{2,3},{3,2},{4,5},{5,4},{6,7},{7,6},{8,9},{9,8},{10,11... | collective-permute-start | bytes 3538952 | tf_op jit(solution)/shard_map/ppermute | solution.py:247
  97.6 1.5 collective-permute-start.10
  101.0 1.3 reduce.3
  107.3 1.4 concatenate.25
  108.7 2.0 %bitcast_add_fusion.8 = f32[2,2,32,1024]{3,2,1,0:T(8,128)} fusion(bf16[2,2,32,1024]{3,2,1,0:T(8,128)(2,1)} %collective-permute-done.10, f32[2,2,2,32,1024]{4,3,2,1,0:T(8,128)} %copy-done.33, s32[]{:T(128)S(6)} %select_n.122), kind=kLoop, calls=%fused_computation.49 | loop fusion | flops 262144 | bytes 1310724 | tf_op jit(solution)/shard_map/add | solution.py:254
  111.9 2.3 %bitcast_add_fusion = f32[2,2,2,2,32,1152]{5,4,2,3,1,0:T(8,128)S(1)} fusion(bf16[2,2,2,2,32,1152]{5,4,2,3,1,0:T(8,128)(2,1)} %collective-permute-done.8, f32[2,2,2,2,2,32,1152]{6,5,4,3,2,1,0:T(8,128)} %bitcast.26, s32[]{:T(128)S(6)} %select_n.120), kind=kLoop, calls=%fused_computation.2 | loop fusion | flops 1179648 | bytes 5898244 | tf_op jit(solution)/shard_map/add | solution.py:254
  118.0 4.1 %all-to-all-start.3 = ((bf16[4,32,2064]{2,1,0:T(8,128)(2,1)}), bf16[4,32,2064]{2,1,0:T(8,128)(2,1)}, u32[]{:S(2)}, u32[]{:S(2)}) async-start(bf16[4,32,2064]{2,1,0:T(8,128)(2,1)} %bitcast.151), calls=%async_computation.3 | async-start | bytes 1114112 | tf_op jit(solution)/shard_map/all_to_all | solution.py:238
  123.4 2.0 %collective-permute-start.13 = (bf16[2,2,2,32,512]{4,3,1,2,0:T(8,128)(2,1)S(1)}, bf16[2,2,2,32,512]{4,3,1,2,0:T(8,128)(2,1)S(1)}, u32[]{:S(2)}, u32[]{:S(2)}) collective-permute-start(bf16[2,2,2,32,512]{4,3,1,2,0:T(8,128)(2,1)S(1)} %fusion.37), channel_id=1, source_target_pairs={{0,8},{8,0},{16,24},{24,16},{1,9},{9,1},{17,25},{25,17},{2,10},{10... | collective-permute-start | bytes 786440 | tf_op jit(solution)/shard_map/ppermute | solution.py:247
  126.5 2.3 %collective-permute-start.11 = (bf16[2,32,2064]{2,1,0:T(8,128)(2,1)S(1)}, bf16[2,32,2064]{2,1,0:T(8,128)(2,1)S(1)}, u32[]{:S(2)}, u32[]{:S(2)}) collective-permute-start(bf16[2,32,2064]{2,1,0:T(8,128)(2,1)S(1)} %fusion.35), channel_id=1, source_target_pairs={{0,2},{1,3},{2,0},{3,1},{4,6},{5,7},{6,4},{7,5},{8,10},{9,11},{10,... | collective-permute-start | bytes 792584 | tf_op jit(solution)/shard_map/ppermute | solution.py:247
  128.8 1.5 collective-permute-start.14
  130.3 5.6 %collective-permute-done.13 = bf16[2,2,2,32,512]{4,3,1,2,0:T(8,128)(2,1)S(1)} collective-permute-done((bf16[2,2,2,32,512]{4,3,1,2,0:T(8,128)(2,1)S(1)}, bf16[2,2,2,32,512]{4,3,1,2,0:T(8,128)(2,1)S(1)}, u32[]{:S(2)}, u32[]{:S(2)}) %collective-permute-start.13) | collective-permute-done | bytes 262176 | tf_op jit(solution)/shard_map/ppermute | solution.py:247
  138.1 3.8 %collective-permute-start.12 = (bf16[32,2064]{1,0:T(8,128)(2,1)}, bf16[32,2064]{1,0:T(8,128)(2,1)}, u32[]{:S(2)}, u32[]{:S(2)}) collective-permute-start(bf16[32,2064]{1,0:T(8,128)(2,1)} %fusion.48), channel_id=1, source_target_pairs={{0,4},{1,5},{2,6},{3,7},{4,0},{5,1},{6,2},{7,3},{8,12},{9,13},{10,... | collective-permute-start | bytes 396296 | tf_op jit(solution)/shard_map/ppermute | solution.py:247
  142.8 1.5 collective-permute-start.15
  146.1 1.6 collective-permute-start.20
  147.7 1.3 copy.77
  150.4 2.4 %fusion.3 = f32[128,1024]{1,0:T(8,128)S(1)} fusion(bf16[1024,2176]{1,0:T(8,128)(2,1)} %param.12, bf16[128,2064]{1,0:T(8,128)(2,1)S(1)} %reshape_reshape.19), kind=kOutput, calls=%fused_computation.10 | convolution fusion | flops 268435456 | bytes 2883584 | tf_op jit(solution)/shard_map/dot_general | solution.py:20
  152.9 2.7 %fusion.7 = f32[128,1024]{1,0:T(8,128)S(1)} fusion(f32[128,1024]{1,0:T(8,128)S(1)} %fusion.3, bf16[128,1152]{1,0:T(8,128)(2,1)S(1)} %bitcast.141, bf16[1024,2176]{1,0:T(8,128)(2,1)} %param.12), kind=kOutput, calls=%fused_computation.19 | convolution fusion | flops 302120960 | bytes 3702784 | tf_op jit(solution)/shard_map/dot_general | solution.py:20
  159.7 4.2 %collective-permute-done.21 = f32[12592]{0:T(1024)S(1)} collective-permute-done((f32[12592]{0:T(1024)S(1)}, f32[12592]{0:T(1024)S(1)}, u32[]{:S(2)}, u32[]{:S(2)}) %collective-permute-start.21) | collective-permute-done | bytes 50400 | tf_op jit(solution)/shard_map/ppermute | solution.py:247
  163.9 1.6 collective-permute-start.22
  166.5 1.5 collective-permute-done.22
  170.6 1.6 collective-permute-done.23
  174.9 3.5 %collective-permute-done.18 = bf16[32,1152]{1,0:T(8,128)(2,1)S(1)} collective-permute-done((bf16[32,1152]{1,0:T(8,128)(2,1)S(1)}, bf16[32,1152]{1,0:T(8,128)(2,1)S(1)}, u32[]{:S(2)}, u32[]{:S(2)}) %collective-permute-start.18) | collective-permute-done | bytes 73760 | tf_op jit(solution)/shard_map/ppermute | solution.py:247
  (216 shorter events, 56.7 us)
Async XLA Ops:
  0.6 24.7 %copy-start = (bf16[1024,1024]{1,0:T(8,128)(2,1)S(1)}, bf16[1024,1024]{1,0:T(8,128)(2,1)}, u32[]{:S(2)}) copy-start(bf16[1024,1024]{1,0:T(8,128)(2,1)} %param.20) | copy-start | bytes 6291460
  1.9 6.9 %copy-start.42 = (bf16[8,2,8,1024]{3,2,1,0:T(8,128)(2,1)S(1)}, bf16[8,2,8,1024]{3,2,1,0:T(8,128)(2,1)}, u32[]{:S(2)}) copy-start(bf16[8,2,8,1024]{3,2,1,0:T(8,128)(2,1)} %param.11) | copy-start | bytes 786436
  3.6 15.4 %all-to-all-start.1 = ((bf16[4,32,2048]{2,1,0:T(8,128)(2,1)}), bf16[4,32,2048]{2,1,0:T(8,128)(2,1)}, u32[]{:S(2)}, u32[]{:S(2)}) async-start(bf16[4,32,2048]{2,1,0:T(8,128)(2,1)} %copy.66), calls=%async_computation.1 | async-start | bytes 1048576 | tf_op jit(solution)/shard_map/all_to_all | solution.py:230
  8.8 6.7 %copy-start.50 = (f32[1152]{0:T(1024)S(1)}, f32[1152]{0:T(1024)}, u32[]{:S(2)}) copy-start(f32[1152]{0:T(1024)} %param.17) | copy-start | bytes 13828
  8.8 6.7 %copy-start.51 = (f32[16]{0:T(128)S(1)}, f32[16]{0:T(128)}, u32[]{:S(2)}) copy-start(f32[16]{0:T(128)} %param.18) | copy-start | bytes 196
  8.8 6.9 %copy-start.45 = (f32[3,3,1152]{2,1,0:T(4,128)S(1)}, f32[3,3,1152]{2,1,0:T(4,128)}, u32[]{:S(2)}) copy-start(f32[3,3,1152]{2,1,0:T(4,128)} %param.16) | copy-start | bytes 124420
  11.0 12.2 %copy-start.46 = (bf16[1024,16]{0,1:T(8,128)(2,1)S(1)}, bf16[1024,16]{0,1:T(8,128)(2,1)}, u32[]{:S(2)}) copy-start(bf16[1024,16]{0,1:T(8,128)(2,1)} %param.13) | copy-start | bytes 98308
  11.0 12.2 %copy-start.52 = (f32[16]{0:T(128)S(1)}, f32[16]{0:T(128)}, u32[]{:S(2)}) copy-start(f32[16]{0:T(128)} %param.14) | copy-start | bytes 196
  11.0 13.9 %copy-start.53 = (f32[16]{0:T(128)S(1)}, f32[16]{0:T(128)}, u32[]{:S(2)}) copy-start(f32[16]{0:T(128)} %param.15) | copy-start | bytes 196
  11.1 4.6 %collective-permute-start.1 = (bf16[8,1,8,1152]{3,2,1,0:T(8,128)(2,1)S(1)}, bf16[8,1,8,1152]{3,2,1,0:T(8,128)(2,1)S(1)}, u32[]{:S(2)}, u32[]{:S(2)}) collective-permute-start(bf16[8,1,8,1152]{3,2,1,0:T(8,128)(2,1)S(1)} %get-tuple-element.113), channel_id=1, source_target_pairs={{1,0},{2,1},{3,2},{4,3},{5,4},{6,5},{7,6},{9,8},{10,9},{11,10},{12... | collective-permute-start | bytes 442376 | tf_op jit(solution)/shard_map/ppermute | solution.py:220
  12.4 4.0 %collective-permute-start = (bf16[8,1,8,1152]{3,2,1,0:T(8,128)(2,1)S(1)}, bf16[8,1,8,1152]{3,2,1,0:T(8,128)(2,1)S(1)}, u32[]{:S(2)}, u32[]{:S(2)}) collective-permute-start(bf16[8,1,8,1152]{3,2,1,0:T(8,128)(2,1)S(1)} %get-tuple-element.114), channel_id=1, source_target_pairs={{0,1},{1,2},{2,3},{3,4},{4,5},{5,6},{6,7},{8,9},{9,10},{10,11},{11... | collective-permute-start | bytes 442376 | tf_op jit(solution)/shard_map/ppermute | solution.py:219
  15.7 11.5 %copy-start.54 = (s32[128]{0:T(128)}, s32[128]{0:T(128)S(1)}, u32[]{:S(2)}) copy-start(s32[128]{0:T(128)S(1)} %and_select_fusion) | copy-start | bytes 1540
  16.4 8.8 %copy-start.7 = (bf16[8,1,8,1152]{3,2,1,0:T(8,128)(2,1)}, bf16[8,1,8,1152]{3,2,1,0:T(8,128)(2,1)S(1)}, u32[]{:S(2)}) copy-start(bf16[8,1,8,1152]{3,2,1,0:T(8,128)(2,1)S(1)} %collective-permute-done.low_ref) | copy-start | bytes 442372
  19.0 11.0 %all-to-all-start = ((bf16[4,32,1152]{2,1,0:T(8,128)(2,1)}), bf16[4,32,1152]{2,1,0:T(8,128)(2,1)S(1)}, u32[]{:S(2)}, u32[]{:S(2)}) async-start(bf16[4,32,1152]{2,1,0:T(8,128)(2,1)} %reshape.142), calls=%async_computation | async-start | bytes 589824 | tf_op jit(solution)/shard_map/all_to_all | solution.py:230
  25.0 5.0 %copy-start.55 = (f32[128,16]{0,1:T(8,128)}, f32[128,16]{0,1:T(8,128)S(1)}, u32[]{:S(2)}) copy-start(f32[128,16]{0,1:T(8,128)S(1)} %get-tuple-element.122) | copy-start | bytes 24580
  46.8 18.0 %collective-permute-start.3 = (bf16[2,2,2,2,32,1024]{5,4,3,2,1,0:T(8,128)(2,1)}, bf16[2,2,2,2,32,1024]{5,4,3,2,1,0:T(8,128)(2,1)}, u32[]{:S(2)}, u32[]{:S(2)}) collective-permute-start(bf16[2,2,2,2,32,1024]{5,4,3,2,1,0:T(8,128)(2,1)} %fusion.16), channel_id=1, source_target_pairs={{0,1},{1,0},{2,3},{3,2},{4,5},{5,4},{6,7},{7,6},{8,9},{9,8},{10,11... | collective-permute-start | bytes 3145736 | tf_op jit(solution)/shard_map/ppermute | solution.py:247
  54.4 12.9 %collective-permute-start.2 = (bf16[2,2,2,2,32,1040]{5,4,3,2,1,0:T(8,128)(2,1)}, bf16[2,2,2,2,32,1040]{5,4,3,2,1,0:T(8,128)(2,1)}, u32[]{:S(2)}, u32[]{:S(2)}) collective-permute-start(bf16[2,2,2,2,32,1040]{5,4,3,2,1,0:T(8,128)(2,1)} %fusion.14), channel_id=1, source_target_pairs={{0,1},{1,0},{2,3},{3,2},{4,5},{5,4},{6,7},{7,6},{8,9},{9,8},{10,11... | collective-permute-start | bytes 3194888 | tf_op jit(solution)/shard_map/ppermute | solution.py:247
  54.4 10.1 %all-to-all-start.2 = ((bf16[4,32,1152]{2,1,0:T(8,128)(2,1)}), bf16[4,32,1152]{2,1,0:T(8,128)(2,1)S(1)}, u32[]{:S(2)}, u32[]{:S(2)}) async-start(bf16[4,32,1152]{2,1,0:T(8,128)(2,1)} %bitcast.10), calls=%async_computation.2 | async-start | bytes 589824 | tf_op jit(solution)/shard_map/all_to_all | solution.py:238
  70.6 13.5 %collective-permute-start.7 = (bf16[2,2,2,32,1024]{4,3,2,1,0:T(8,128)(2,1)}, bf16[2,2,2,32,1024]{4,3,2,1,0:T(8,128)(2,1)}, u32[]{:S(2)}, u32[]{:S(2)}) collective-permute-start(bf16[2,2,2,32,1024]{4,3,2,1,0:T(8,128)(2,1)} %fusion.23), channel_id=1, source_target_pairs={{0,16},{8,24},{16,0},{24,8},{1,17},{9,25},{17,1},{25,9},{2,18},{10... | collective-permute-start | bytes 1572872 | tf_op jit(solution)/shard_map/ppermute | solution.py:247
  73.0 14.7 %collective-permute-start.6 = (bf16[2,2,2,32,1040]{4,3,2,1,0:T(8,128)(2,1)}, bf16[2,2,2,32,1040]{4,3,2,1,0:T(8,128)(2,1)}, u32[]{:S(2)}, u32[]{:S(2)}) collective-permute-start(bf16[2,2,2,32,1040]{4,3,2,1,0:T(8,128)(2,1)} %fusion.17), channel_id=1, source_target_pairs={{0,8},{8,0},{16,24},{24,16},{1,9},{9,1},{17,25},{25,17},{2,10},{10... | collective-permute-start | bytes 1597448 | tf_op jit(solution)/shard_map/ppermute | solution.py:247
  74.5 4.5 %collective-permute-start.5 = (bf16[8,1,8,1152]{3,2,1,0:T(8,128)(2,1)}, bf16[8,1,8,1152]{3,2,1,0:T(8,128)(2,1)S(1)}, u32[]{:S(2)}, u32[]{:S(2)}) collective-permute-start(bf16[8,1,8,1152]{3,2,1,0:T(8,128)(2,1)} %get-tuple-element.111), channel_id=1, source_target_pairs={{1,0},{2,1},{3,2},{4,3},{5,4},{6,5},{7,6},{9,8},{10,9},{11,10},{12... | collective-permute-start | bytes 442376 | tf_op jit(solution)/shard_map/ppermute | solution.py:220
  75.8 4.2 %collective-permute-start.4 = (bf16[8,1,8,1152]{3,2,1,0:T(8,128)(2,1)}, bf16[8,1,8,1152]{3,2,1,0:T(8,128)(2,1)S(1)}, u32[]{:S(2)}, u32[]{:S(2)}) collective-permute-start(bf16[8,1,8,1152]{3,2,1,0:T(8,128)(2,1)} %get-tuple-element.112), channel_id=1, source_target_pairs={{0,1},{1,2},{2,3},{3,4},{4,5},{5,6},{6,7},{8,9},{9,10},{10,11},{11... | collective-permute-start | bytes 442376 | tf_op jit(solution)/shard_map/ppermute | solution.py:219
  85.6 11.3 %copy-start.33 = (f32[2,2,2,32,1024]{4,3,2,1,0:T(8,128)}, f32[2,2,2,32,1024]{4,3,2,1,0:T(8,128)S(1)}, u32[]{:S(2)}) copy-start(f32[2,2,2,32,1024]{4,3,2,1,0:T(8,128)S(1)} %bitcast_add_fusion.4) | copy-start | bytes 3145732
  88.8 10.3 %copy-start.32 = (f32[2,2,2,32,1040]{4,3,2,1,0:T(8,128)}, f32[2,2,2,32,1040]{4,3,2,1,0:T(8,128)S(1)}, u32[]{:S(2)}) copy-start(f32[2,2,2,32,1040]{4,3,2,1,0:T(8,128)S(1)} %bitcast_add_fusion.3) | copy-start | bytes 3194884
  91.9 9.1 %copy-start.21 = (f32[1,1024]{1,0:T(1,128)S(1)}, f32[1,1024]{1,0:T(1,128)}, u32[]{:S(2)}) copy-start(f32[1,1024]{1,0:T(1,128)} %copy-done.20) | copy-start | bytes 12292
  91.9 15.4 %copy-start.23 = (f32[1,1024]{1,0:T(1,128)S(1)}, f32[1,1024]{1,0:T(1,128)}, u32[]{:S(2)}) copy-start(f32[1,1024]{1,0:T(1,128)} %copy-done.22) | copy-start | bytes 12292
  94.8 17.2 %collective-permute-start.8 = (bf16[2,2,2,2,32,1152]{5,4,2,3,1,0:T(8,128)(2,1)}, bf16[2,2,2,2,32,1152]{5,4,2,3,1,0:T(8,128)(2,1)}, u32[]{:S(2)}, u32[]{:S(2)}) collective-permute-start(bf16[2,2,2,2,32,1152]{5,4,2,3,1,0:T(8,128)(2,1)} %fusion.15), channel_id=1, source_target_pairs={{0,1},{1,0},{2,3},{3,2},{4,5},{5,4},{6,7},{7,6},{8,9},{9,8},{10,11... | collective-permute-start | bytes 3538952 | tf_op jit(solution)/shard_map/ppermute | solution.py:247
  97.6 11.1 %collective-permute-start.10 = (bf16[2,2,32,1024]{3,2,1,0:T(8,128)(2,1)}, bf16[2,2,32,1024]{3,2,1,0:T(8,128)(2,1)}, u32[]{:S(2)}, u32[]{:S(2)}) collective-permute-start(bf16[2,2,32,1024]{3,2,1,0:T(8,128)(2,1)} %fusion.36), channel_id=1, source_target_pairs={{0,8},{8,0},{16,24},{24,16},{1,9},{9,1},{17,25},{25,17},{2,10},{10... | collective-permute-start | bytes 786440 | tf_op jit(solution)/shard_map/ppermute | solution.py:247
  99.8 10.9 %collective-permute-start.9 = (bf16[2,2,32,1040]{3,2,1,0:T(8,128)(2,1)}, bf16[2,2,32,1040]{3,2,1,0:T(8,128)(2,1)}, u32[]{:S(2)}, u32[]{:S(2)}) collective-permute-start(bf16[2,2,32,1040]{3,2,1,0:T(8,128)(2,1)} %fusion.25), channel_id=1, source_target_pairs={{0,16},{8,24},{16,0},{24,8},{1,17},{9,25},{17,1},{25,9},{2,18},{10... | collective-permute-start | bytes 798728 | tf_op jit(solution)/shard_map/ppermute | solution.py:247
  118.0 29.8 %all-to-all-start.3 = ((bf16[4,32,2064]{2,1,0:T(8,128)(2,1)}), bf16[4,32,2064]{2,1,0:T(8,128)(2,1)}, u32[]{:S(2)}, u32[]{:S(2)}) async-start(bf16[4,32,2064]{2,1,0:T(8,128)(2,1)} %bitcast.151), calls=%async_computation.3 | async-start | bytes 1114112 | tf_op jit(solution)/shard_map/all_to_all | solution.py:238
  122.1 6.6 %copy-start.31 = (f32[2,2,2,2,32,640]{5,4,2,3,1,0:T(8,128)S(1)}, f32[2,2,2,2,32,640]{5,4,2,3,1,0:T(8,128)}, u32[]{:S(2)}) copy-start(f32[2,2,2,2,32,640]{5,4,2,3,1,0:T(8,128)} %slice.81) | copy-start | bytes 3932164
  122.1 15.0 %copy-start.30 = (f32[2,2,32,1024]{3,2,1,0:T(8,128)S(1)}, f32[2,2,32,1024]{3,2,1,0:T(8,128)}, u32[]{:S(2)}) copy-start(f32[2,2,32,1024]{3,2,1,0:T(8,128)} %bitcast_add_fusion.8) | copy-start | bytes 1572868
  123.4 12.6 %collective-permute-start.13 = (bf16[2,2,2,32,512]{4,3,1,2,0:T(8,128)(2,1)S(1)}, bf16[2,2,2,32,512]{4,3,1,2,0:T(8,128)(2,1)S(1)}, u32[]{:S(2)}, u32[]{:S(2)}) collective-permute-start(bf16[2,2,2,32,512]{4,3,1,2,0:T(8,128)(2,1)S(1)} %fusion.37), channel_id=1, source_target_pairs={{0,8},{8,0},{16,24},{24,16},{1,9},{9,1},{17,25},{25,17},{2,10},{10... | collective-permute-start | bytes 786440 | tf_op jit(solution)/shard_map/ppermute | solution.py:247
  126.5 10.7 %collective-permute-start.11 = (bf16[2,32,2064]{2,1,0:T(8,128)(2,1)S(1)}, bf16[2,32,2064]{2,1,0:T(8,128)(2,1)S(1)}, u32[]{:S(2)}, u32[]{:S(2)}) collective-permute-start(bf16[2,32,2064]{2,1,0:T(8,128)(2,1)S(1)} %fusion.35), channel_id=1, source_target_pairs={{0,2},{1,3},{2,0},{3,1},{4,6},{5,7},{6,4},{7,5},{8,10},{9,11},{10,... | collective-permute-start | bytes 792584 | tf_op jit(solution)/shard_map/ppermute | solution.py:247
  128.8 13.0 %collective-permute-start.14 = (bf16[2,2,2,32,640]{4,3,1,2,0:T(8,128)(2,1)S(1)}, bf16[2,2,2,32,640]{4,3,1,2,0:T(8,128)(2,1)S(1)}, u32[]{:S(2)}, u32[]{:S(2)}) collective-permute-start(bf16[2,2,2,32,640]{4,3,1,2,0:T(8,128)(2,1)S(1)} %fusion.24), channel_id=1, source_target_pairs={{0,16},{8,24},{16,0},{24,8},{1,17},{9,25},{17,1},{25,9},{2,18},{10... | collective-permute-start | bytes 983048 | tf_op jit(solution)/shard_map/ppermute | solution.py:247
  137.1 7.9 %copy-start.38 = (f32[2,2,2,32,512]{4,3,1,2,0:T(8,128)}, f32[2,2,2,32,512]{4,3,1,2,0:T(8,128)S(1)}, u32[]{:S(2)}) copy-start(f32[2,2,2,32,512]{4,3,1,2,0:T(8,128)S(1)} %bitcast_add_fusion.7) | copy-start | bytes 1572868
  138.1 17.5 %collective-permute-start.12 = (bf16[32,2064]{1,0:T(8,128)(2,1)}, bf16[32,2064]{1,0:T(8,128)(2,1)}, u32[]{:S(2)}, u32[]{:S(2)}) collective-permute-start(bf16[32,2064]{1,0:T(8,128)(2,1)} %fusion.48), channel_id=1, source_target_pairs={{0,4},{1,5},{2,6},{3,7},{4,0},{5,1},{6,2},{7,3},{8,12},{9,13},{10,... | collective-permute-start | bytes 396296 | tf_op jit(solution)/shard_map/ppermute | solution.py:247
  141.9 3.6 %collective-permute-start.19 = (f32[12592]{0:T(1024)S(1)}, f32[12592]{0:T(1024)S(1)}, u32[]{:S(2)}, u32[]{:S(2)}) collective-permute-start(f32[12592]{0:T(1024)S(1)} %copy-done.44), channel_id=1, source_target_pairs={{0,1},{1,0},{2,3},{3,2},{4,5},{5,4},{6,7},{7,6},{8,9},{9,8},{10,11... | collective-permute-start | bytes 151112 | tf_op jit(solution)/shard_map/ppermute | solution.py:247
  142.8 15.9 %collective-permute-start.15 = (bf16[2,2,32,512]{3,2,0,1:T(8,128)(2,1)}, bf16[2,2,32,512]{3,2,0,1:T(8,128)(2,1)}, u32[]{:S(2)}, u32[]{:S(2)}) collective-permute-start(bf16[2,2,32,512]{3,2,0,1:T(8,128)(2,1)} %fusion.49), channel_id=1, source_target_pairs={{0,16},{8,24},{16,0},{24,8},{1,17},{9,25},{17,1},{25,9},{2,18},{10... | collective-permute-start | bytes 393224 | tf_op jit(solution)/shard_map/ppermute | solution.py:247
  145.0 20.5 %collective-permute-start.16 = (bf16[2,2,32,640]{3,2,0,1:T(8,128)(2,1)}, bf16[2,2,32,640]{3,2,0,1:T(8,128)(2,1)}, u32[]{:S(2)}, u32[]{:S(2)}) collective-permute-start(bf16[2,2,32,640]{3,2,0,1:T(8,128)(2,1)} %fusion.46), channel_id=1, source_target_pairs={{0,8},{8,0},{16,24},{24,16},{1,9},{9,1},{17,25},{25,17},{2,10},{10... | collective-permute-start | bytes 491528 | tf_op jit(solution)/shard_map/ppermute | solution.py:247
  146.1 11.3 %collective-permute-start.20 = (f32[12592]{0:T(1024)}, f32[12592]{0:T(1024)}, u32[]{:S(2)}, u32[]{:S(2)}) collective-permute-start(f32[12592]{0:T(1024)} %add.223), channel_id=1, source_target_pairs={{0,2},{1,3},{2,0},{3,1},{4,6},{5,7},{6,4},{7,5},{8,10},{9,11},{10,... | collective-permute-start | bytes 151112 | tf_op jit(solution)/shard_map/ppermute | solution.py:247
  152.8 5.9 %copy-start.39 = (f32[2,2,2,32,512]{4,3,1,2,0:T(8,128)S(1)}, f32[2,2,2,32,512]{4,3,1,2,0:T(8,128)}, u32[]{:S(2)}) copy-start(f32[2,2,2,32,512]{4,3,1,2,0:T(8,128)} %copy-done.38) | copy-start | bytes 1572868
  155.5 9.9 %copy-start.35 = (f32[2,2,2,32,640]{4,3,1,2,0:T(8,128)S(1)}, f32[2,2,2,32,640]{4,3,1,2,0:T(8,128)}, u32[]{:S(2)}) copy-start(f32[2,2,2,32,640]{4,3,1,2,0:T(8,128)} %copy-done.34) | copy-start | bytes 1966084
  158.3 5.5 %collective-permute-start.21 = (f32[12592]{0:T(1024)S(1)}, f32[12592]{0:T(1024)S(1)}, u32[]{:S(2)}, u32[]{:S(2)}) collective-permute-start(f32[12592]{0:T(1024)S(1)} %add.224), channel_id=1, source_target_pairs={{0,4},{1,5},{2,6},{3,7},{4,0},{5,1},{6,2},{7,3},{8,12},{9,13},{10,... | collective-permute-start | bytes 151112 | tf_op jit(solution)/shard_map/ppermute | solution.py:247
  163.9 4.2 %collective-permute-start.22 = (f32[12592]{0:T(1024)S(1)}, f32[12592]{0:T(1024)S(1)}, u32[]{:S(2)}, u32[]{:S(2)}) collective-permute-start(f32[12592]{0:T(1024)S(1)} %add.225), channel_id=1, source_target_pairs={{0,8},{8,0},{16,24},{24,16},{1,9},{9,1},{17,25},{25,17},{2,10},{10... | collective-permute-start | bytes 151112 | tf_op jit(solution)/shard_map/ppermute | solution.py:247
  166.4 5.9 %collective-permute-start.17 = (bf16[2,32,1152]{2,1,0:T(8,128)(2,1)S(1)}, bf16[2,32,1152]{2,1,0:T(8,128)(2,1)S(1)}, u32[]{:S(2)}, u32[]{:S(2)}) collective-permute-start(bf16[2,32,1152]{2,1,0:T(8,128)(2,1)S(1)} %fusion.47), channel_id=1, source_target_pairs={{0,2},{1,3},{2,0},{3,1},{4,6},{5,7},{6,4},{7,5},{8,10},{9,11},{10,... | collective-permute-start | bytes 442376 | tf_op jit(solution)/shard_map/ppermute | solution.py:247
  168.1 4.2 %collective-permute-start.23 = (f32[12592]{0:T(1024)S(1)}, f32[12592]{0:T(1024)S(1)}, u32[]{:S(2)}, u32[]{:S(2)}) collective-permute-start(f32[12592]{0:T(1024)S(1)} %add.226), channel_id=1, source_target_pairs={{0,16},{8,24},{16,0},{24,8},{1,17},{9,25},{17,1},{25,9},{2,18},{10... | collective-permute-start | bytes 151112 | tf_op jit(solution)/shard_map/ppermute | solution.py:247
  172.4 6.0 %collective-permute-start.18 = (bf16[32,1152]{1,0:T(8,128)(2,1)S(1)}, bf16[32,1152]{1,0:T(8,128)(2,1)S(1)}, u32[]{:S(2)}, u32[]{:S(2)}) collective-permute-start(bf16[32,1152]{1,0:T(8,128)(2,1)S(1)} %fusion.50), channel_id=1, source_target_pairs={{0,4},{1,5},{2,6},{3,7},{4,0},{5,1},{6,2},{7,3},{8,12},{9,13},{10,... | collective-permute-start | bytes 221192 | tf_op jit(solution)/shard_map/ppermute | solution.py:247
  (36 other events, 76.2 us)
